TPU v7x, 256 devices: a whole 4x4x8 slice. The times are simulated.
256 devices in a mesh: tm: 16 (over x_hi, y, core), space: 16 (over z, x_lo).
Axes of the slice: x: 4 (x_hi: 2, x_lo: 2; x = x_hi * 2 + x_lo), y: 4, z: 8, core: 2. Of those that a mesh axis runs over, the one named last changes fastest.
Arguments:
- queries: bfloat16 [16, 16, 128, 1536], P('tm', 'space'), may hold values from -100 to 100
- key_states: bfloat16 [16, 16, 128, 1536], P('tm', 'space'), may hold values from -4.5 to 4.5
- value_states: bfloat16 [16, 16, 128, 1536], P('tm', 'space'), may hold values from -6 to 6
- grad_out: bfloat16 [16, 16, 128, 1536], P('tm', 'space'), may hold values from -6 to 6
- window: int32 [16, 16, 2, 27], P('tm', 'space'), may hold values 0 or 1
Outputs:
- grad_queries: bfloat16 [16, 16, 128, 1536], P('tm', 'space')
- grad_keys: bfloat16 [16, 16, 128, 1536], P('tm', 'space')
- grad_values: bfloat16 [16, 16, 128, 1536], P('tm', 'space')
All inputs are finite; a program needn't handle non-finite values. No bound on the sum of `window` on one device may be relied on, other than what follows from the above.
Results may differ from a plain program's by a relative error of at most 0.011.
Values may be sent and summed in bfloat16 or wider, within the bound.
A program may use at most 64 MiB of HBM per device.

v0:
```python
import jax
import jax.numpy as jnp
from jax import lax
from jax.sharding import PartitionSpec as P

HEADS = 12
HEAD_DIM = 128
TILE_TOKENS = 64


CROSS = ((0, 1), (1, 0), (1, 1), (1, 2), (2, 1))


def with_halo(block, sides, width):
    for axis, dim in sides:
        count = lax.axis_size(axis)
        forward = [(i, i + 1) for i in range(count - 1)]
        backward = [(target, source) for source, target in forward]
        low = lax.ppermute(
            lax.slice_in_dim(block, block.shape[dim] - width, None, axis=dim), axis, forward
        )
        high = lax.ppermute(lax.slice_in_dim(block, 0, width, axis=dim), axis, backward)
        block = jnp.concatenate([low, block, high], axis=dim)
    return block


def passed_along(value, axis, steps):
    count = lax.axis_size(axis)
    first, last = (max(0, -steps), min(count, count - steps))
    return lax.ppermute(value, axis, [(source, source + steps) for source in range(first, last)])


def split_heads(token_rows):
    return token_rows.reshape(token_rows.shape[0], HEADS, HEAD_DIM)


def inside(position, offset_step, extent):
    return (position + offset_step >= 0) & (position + offset_step < extent)


def tile_allow(listed, frame_step, band_step, present):
    tile_count = listed.shape[0]
    query_tile = jnp.arange(tile_count)[:, None]
    key_tile = jnp.arange(tile_count)[None, :]
    column_step = key_tile - query_tile
    offset_code = (frame_step + 1) * 9 + (band_step + 1) * 3 + jnp.clip(column_step, -1, 1) + 1
    onehot = offset_code[:, :, None] == jnp.arange(27)[None, None, :]
    chosen = jnp.sum(jnp.where(onehot, listed[:, None, :], 0), axis=2) > 0
    centre = (frame_step == 0) & (band_step == 0) & (column_step == 0)
    return present & (jnp.abs(column_step) <= 1) & (chosen | centre)


def expand(allowed):
    return jnp.repeat(jnp.repeat(allowed, TILE_TOKENS, axis=0), TILE_TOKENS, axis=1)


def cross_blocks(grid):
    return jnp.stack([grid[f, b] for f, b in CROSS])


def body(queries, key_states, value_states, grad_out, window):
    block_rows = queries.shape[2]
    feature_count = queries.shape[3]
    score_scale = HEAD_DIM ** (-0.5)
    slab_index = lax.axis_index("tm")
    band_index = lax.axis_index("space")
    slab_count = lax.axis_size("tm")
    band_count = lax.axis_size("space")
    packed = jnp.concatenate([key_states, value_states], axis=3)
    nearby = cross_blocks(with_halo(packed, (("tm", 0), ("space", 1)), 1))
    key_heads = split_heads(nearby[:, :, :feature_count].reshape(5 * block_rows, feature_count))
    value_heads = split_heads(nearby[:, :, feature_count:].reshape(5 * block_rows, feature_count))
    query_heads = split_heads(queries[0, 0])
    grad_heads = split_heads(grad_out[0, 0])
    pieces = []
    for frame_pos, band_pos in CROSS:
        present = inside(slab_index, frame_pos - 1, slab_count) & inside(
            band_index, band_pos - 1, band_count
        )
        pieces.append(tile_allow(window[0, 0], frame_pos - 1, band_pos - 1, present))
    allowed = expand(jnp.concatenate(pieces, axis=1))
    scores = (
        jnp.einsum("qhd,khd->hqk", query_heads, key_heads, preferred_element_type=jnp.float32)
        * score_scale
    )
    scores = jnp.where(allowed[None], scores, -1e30)
    row_top = jnp.max(scores, axis=2, keepdims=True)
    weight = jnp.exp(scores - row_top)
    row_total = jnp.sum(weight, axis=2, keepdims=True)
    prob_full = weight / row_total
    prob_low = prob_full.astype(jnp.bfloat16)
    attended = jnp.einsum("hqk,khd->qhd", prob_low, value_heads, preferred_element_type=jnp.float32)
    row_delta = jnp.sum(grad_heads.astype(jnp.float32) * attended, axis=2).T[:, :, None]
    grad_probs = jnp.einsum(
        "qhd,khd->hqk", grad_heads, value_heads, preferred_element_type=jnp.float32
    )
    grad_scores = (prob_full * (grad_probs - row_delta) * score_scale).astype(jnp.bfloat16)
    query_grad = jnp.einsum(
        "hqk,khd->qhd", grad_scores, key_heads, preferred_element_type=jnp.float32
    )
    grad_queries = query_grad.reshape(block_rows, feature_count).astype(jnp.bfloat16)[None, None]
    key_grad = jnp.einsum(
        "hqk,qhd->khd", grad_scores, query_heads, preferred_element_type=jnp.float32
    )
    value_grad = jnp.einsum(
        "hqk,qhd->khd", prob_low, grad_heads, preferred_element_type=jnp.float32
    )
    partial_value = jnp.concatenate(
        [
            key_grad.reshape(5, block_rows, feature_count),
            value_grad.reshape(5, block_rows, feature_count),
        ],
        axis=2,
    )
    summed = (
        partial_value[2]
        + passed_along(partial_value[1], "space", -1)
        + passed_along(partial_value[3], "space", 1)
    )
    summed = (
        summed + passed_along(partial_value[0], "tm", -1) + passed_along(partial_value[4], "tm", 1)
    )
    grad_keys = summed[:, :feature_count].astype(jnp.bfloat16)[None, None]
    grad_values = summed[:, feature_count:].astype(jnp.bfloat16)[None, None]
    return (grad_queries, grad_keys, grad_values)


def solution(mesh):
    return jax.shard_map(
        body,
        mesh=mesh,
        in_specs=(
            P("tm", "space", None, None),
            P("tm", "space", None, None),
            P("tm", "space", None, None),
            P("tm", "space", None, None),
            P("tm", "space", None, None),
        ),
        out_specs=(
            P("tm", "space", None, None),
            P("tm", "space", None, None),
            P("tm", "space", None, None),
        ),
        check_vma=False,
    )
```

profile of v0, /device:TPU:121, one launch (start us, length us, event | category | flops | bytes accessed | tf_op | source)
XLA Modules:
  0.0 286.2 jit_solution(8471568417288194694)
XLA Ops:
  0.6 1.0 constant_dynamic-update-slice_fusion.1
  1.7 1.0 constant_dynamic-update-slice_fusion
  2.7 2.7 collective-permute-start.1
  5.5 6.6 %collective-permute-start = (bf16[1,1,128,3072]{3,2,1,0:T(8,128)(2,1)S(1)}, bf16[1,1,128,3072]{3,2,1,0:T(8,128)(2,1)S(1)}, u32[]{:S(2)}, u32[]{:S(2)}) collective-permute-start(bf16[1,1,128,3072]{3,2,1,0:T(8,128)(2,1)S(1)} %constant_dynamic-update-slice_fusion), channel_id=1, source_target_pairs={{0,16},{16,32},{32,48},{48,64},{64,80},{80,96},{96,112},{112,128},... | collective-permute-start | bytes 2359304 | tf_op jit(solution)/shard_map/ppermute | solution.py:19
  12.1 7.7 %collective-permute-done.1 = bf16[1,1,128,3072]{3,2,1,0:T(8,128)(2,1)S(1)} collective-permute-done((bf16[1,1,128,3072]{3,2,1,0:T(8,128)(2,1)S(1)}, bf16[1,1,128,3072]{3,2,1,0:T(8,128)(2,1)S(1)}, u32[]{:S(2)}, u32[]{:S(2)}) %collective-permute-start.1) | collective-permute-done | bytes 786464 | tf_op jit(solution)/shard_map/ppermute | solution.py:22
  19.8 1.2 collective-permute-done
  21.0 1.7 pad_maximum_fusion
  22.6 3.1 %collective-permute-start.2 = (bf16[3,1,128,3072]{3,2,1,0:T(8,128)(2,1)}, bf16[3,1,128,3072]{3,2,1,0:T(8,128)(2,1)}, u32[]{:S(2)}, u32[]{:S(2)}) collective-permute-start(bf16[3,1,128,3072]{3,2,1,0:T(8,128)(2,1)} %pad_maximum_fusion), channel_id=1, source_target_pairs={{0,1},{1,2},{2,3},{3,4},{4,5},{5,6},{6,7},{7,8},{8,9},{9,10},{10,1... | collective-permute-start | bytes 7077896 | tf_op jit(solution)/shard_map/ppermute | solution.py:19
  25.9 0.3 fusion.23
  26.2 3.1 %collective-permute-start.3 = (bf16[3,1,128,3072]{3,2,1,0:T(8,128)(2,1)}, bf16[3,1,128,3072]{3,2,1,0:T(8,128)(2,1)}, u32[]{:S(2)}, u32[]{:S(2)}) collective-permute-start(bf16[3,1,128,3072]{3,2,1,0:T(8,128)(2,1)} %pad_maximum_fusion), channel_id=1, source_target_pairs={{1,0},{2,1},{3,2},{4,3},{5,4},{6,5},{7,6},{8,7},{9,8},{10,9},{11,1... | collective-permute-start | bytes 7077896 | tf_op jit(solution)/shard_map/ppermute | solution.py:22
  29.9 1.2 copy.63
  31.2 94.9 %collective-permute-done.2 = bf16[3,1,128,3072]{3,2,1,0:T(8,128)(2,1)} collective-permute-done((bf16[3,1,128,3072]{3,2,1,0:T(8,128)(2,1)}, bf16[3,1,128,3072]{3,2,1,0:T(8,128)(2,1)}, u32[]{:S(2)}, u32[]{:S(2)}) %collective-permute-start.2) | collective-permute-done | bytes 2359328 | tf_op jit(solution)/shard_map/ppermute | solution.py:19
  126.1 1.2 fusion.16
  127.4 0.5 collective-permute-done.3
  127.9 1.2 fusion.15
  129.1 2.2 fusion.32
  131.4 3.7 %reshape_reshape.7 = bf16[640,12,128]{2,1,0:T(8,128)(2,1)S(1)} reshape(bf16[5,128,1536]{2,1,0:T(8,128)(2,1)} %get-tuple-element.24) | data formatting | bytes 3932160 | tf_op jit(solution)/shard_map/reshape;reshape | solution.py:34
  135.1 3.3 %copy.66 = bf16[640,12,128]{0,2,1:T(8,128)(2,1)} copy(bf16[640,12,128]{2,1,0:T(8,128)(2,1)S(1)} %reshape_reshape.7) | data formatting | bytes 3932160 | tf_op jit(solution)/shard_map/reshape;reshape | solution.py:34
  138.4 3.7 %reshape_reshape.6 = bf16[640,12,128]{2,1,0:T(8,128)(2,1)S(1)} reshape(bf16[5,128,1536]{2,1,0:T(8,128)(2,1)} %get-tuple-element.25) | data formatting | bytes 3932160 | tf_op jit(solution)/shard_map/reshape;reshape | solution.py:34
  142.2 3.4 %copy.68 = bf16[640,12,128]{0,2,1:T(8,128)(2,1)} copy(bf16[640,12,128]{2,1,0:T(8,128)(2,1)S(1)} %reshape_reshape.6) | data formatting | bytes 3932160 | tf_op jit(solution)/shard_map/reshape;reshape | solution.py:34
  145.6 5.1 %fusion.33 = (f32[12,128]{1,0:T(8,128)S(1)}, f32[12,128,640]{1,2,0:T(8,128)}) fusion(pred[128,640]{0,1:T(8,128)(4,1)S(1)} %bitcast.95, bf16[640,12,128]{0,2,1:T(8,128)(2,1)} %copy.68, bf16[128,12,128]{0,2,1:T(8,128)(2,1)S(1)} %bitcast.89), kind=kOutput, calls=%fused_computation.69 | convolution fusion | flops 255591040 | bytes 6379520 | tf_op jit(solution)/shard_map/sub | solution.py:88
  150.7 2.5 fusion.7
  153.2 2.6 convolution_bitcast_fusion
  155.8 0.7 fusion.14
  156.5 1.4 copy-done.3
  157.9 1.1 fusion.2
  159.0 0.7 convolution_bitcast_fusion.1
  159.7 4.8 %copy.71 = f32[640,12,128]{2,1,0:T(8,128)} copy(f32[640,12,128]{2,0,1:T(8,128)S(1)} %convolution_bitcast_fusion.1) | data formatting | bytes 7864320 | tf_op jit(solution)/shard_map/hqk,qhd->khd/transpose | solution.py:102
  164.5 5.5 %reshape.87 = f32[5,128,1536]{2,1,0:T(8,128)} reshape(f32[640,12,128]{2,1,0:T(8,128)} %copy.71) | data formatting | bytes 7864320 | tf_op jit(solution)/shard_map/reshape | solution.py:110
  170.0 6.9 %copy.73 = f32[640,12,128]{2,1,0:T(8,128)} copy(f32[640,12,128]{2,0,1:T(8,128)} %convolution_bitcast_fusion) | data formatting | bytes 7864320 | tf_op jit(solution)/shard_map/hqk,qhd->khd/transpose | solution.py:105
  176.9 5.5 %reshape.88 = f32[5,128,1536]{2,1,0:T(8,128)} reshape(f32[640,12,128]{2,1,0:T(8,128)} %copy.73) | data formatting | bytes 7864320 | tf_op jit(solution)/shard_map/reshape | solution.py:111
  182.4 2.5 constant_dynamic-update-slice_fusion.3
  185.0 0.8 copy-done.1
  185.7 0.4 constant_dynamic-update-slice_fusion.2
  186.1 2.2 slice_bitcast_fusion.3
  188.3 2.5 copy-done
  190.8 2.8 collective-permute-start.4
  193.7 2.9 %collective-permute-start.7 = (f32[128,3072]{1,0:T(8,128)}, f32[128,3072]{1,0:T(8,128)}, u32[]{:S(2)}, u32[]{:S(2)}) collective-permute-start(f32[128,3072]{1,0:T(8,128)} %get-tuple-element.21), channel_id=1, source_target_pairs={{0,16},{16,32},{32,48},{48,64},{64,80},{80,96},{96,112},{112,128},... | collective-permute-start | bytes 4718600 | tf_op jit(solution)/shard_map/ppermute | solution.py:30
  196.6 1.9 collective-permute-start.6
  198.5 2.1 collective-permute-start.5
  200.7 1.4 convolution_convert_fusion
  202.1 1.9 copy.74
  204.0 58.3 %collective-permute-done.4 = f32[128,3072]{1,0:T(8,128)} collective-permute-done((f32[128,3072]{1,0:T(8,128)}, f32[128,3072]{1,0:T(8,128)}, u32[]{:S(2)}, u32[]{:S(2)}) %collective-permute-start.4) | collective-permute-done | bytes 1572896 | tf_op jit(solution)/shard_map/ppermute | solution.py:30
  262.3 2.3 collective-permute-done.7
  264.6 1.0 collective-permute-done.6
  265.7 15.8 %collective-permute-done.5 = f32[128,3072]{1,0:T(8,128)} collective-permute-done((f32[128,3072]{1,0:T(8,128)S(1)}, f32[128,3072]{1,0:T(8,128)}, u32[]{:S(2)}, u32[]{:S(2)}) %collective-permute-start.5) | collective-permute-done | bytes 1572896 | tf_op jit(solution)/shard_map/ppermute | solution.py:30
  281.5 3.8 %fusion.12 = bf16[128,3072]{1,0:T(8,128)(2,1)S(1)} fusion(f32[128,3072]{1,0:T(8,128)} %collective-permute-done.7, f32[128,3072]{1,0:T(8,128)} %collective-permute-done.6, f32[128,3072]{1,0:T(8,128)} %collective-permute-done.5, f32[128,3072]{1,0:T(8,128)} %collective-permute-done.4, f32[5,128,3072]{2,1,0:T(8,128)} %copy-done), kind=kLoop, calls=%fused_computation.24 | loop fusion | flops 1966080 | bytes 8650752 | tf_op jit(solution)/shard_map/convert.1
  285.3 0.9 slice_bitcast_fusion.7
  (28 shorter events, 0.9 us)
Async XLA Ops:
  2.7 23.1 %copy-start.6 = (s32[1,1,2,27]{3,2,1,0:T(2,128)S(1)}, s32[1,1,2,27]{3,2,1,0:T(2,128)}, u32[]{:S(2)}) copy-start(s32[1,1,2,27]{3,2,1,0:T(2,128)} %param.9) | copy-start | bytes 652
  2.7 27.0 %copy-start.5 = (bf16[1,1,128,1536]{3,2,1,0:T(8,128)(2,1)S(1)}, bf16[1,1,128,1536]{3,2,1,0:T(8,128)(2,1)}, u32[]{:S(2)}) copy-start(bf16[1,1,128,1536]{3,2,1,0:T(8,128)(2,1)} %param.5) | copy-start | bytes 1179652
  2.7 17.1 %collective-permute-start.1 = (bf16[1,1,128,3072]{3,2,1,0:T(8,128)(2,1)S(1)}, bf16[1,1,128,3072]{3,2,1,0:T(8,128)(2,1)S(1)}, u32[]{:S(2)}, u32[]{:S(2)}) collective-permute-start(bf16[1,1,128,3072]{3,2,1,0:T(8,128)(2,1)S(1)} %constant_dynamic-update-slice_fusion), channel_id=1, source_target_pairs={{16,0},{32,16},{48,32},{64,48},{80,64},{96,80},{112,96},{128,112},... | collective-permute-start | bytes 2359304 | tf_op jit(solution)/shard_map/ppermute | solution.py:22
  5.5 15.5 %collective-permute-start = (bf16[1,1,128,3072]{3,2,1,0:T(8,128)(2,1)S(1)}, bf16[1,1,128,3072]{3,2,1,0:T(8,128)(2,1)S(1)}, u32[]{:S(2)}, u32[]{:S(2)}) collective-permute-start(bf16[1,1,128,3072]{3,2,1,0:T(8,128)(2,1)S(1)} %constant_dynamic-update-slice_fusion), channel_id=1, source_target_pairs={{0,16},{16,32},{32,48},{48,64},{64,80},{80,96},{96,112},{112,128},... | collective-permute-start | bytes 2359304 | tf_op jit(solution)/shard_map/ppermute | solution.py:19
  22.6 103.5 %collective-permute-start.2 = (bf16[3,1,128,3072]{3,2,1,0:T(8,128)(2,1)}, bf16[3,1,128,3072]{3,2,1,0:T(8,128)(2,1)}, u32[]{:S(2)}, u32[]{:S(2)}) collective-permute-start(bf16[3,1,128,3072]{3,2,1,0:T(8,128)(2,1)} %pad_maximum_fusion), channel_id=1, source_target_pairs={{0,1},{1,2},{2,3},{3,4},{4,5},{5,6},{6,7},{7,8},{8,9},{9,10},{10,1... | collective-permute-start | bytes 7077896 | tf_op jit(solution)/shard_map/ppermute | solution.py:19
  26.2 101.7 %collective-permute-start.3 = (bf16[3,1,128,3072]{3,2,1,0:T(8,128)(2,1)}, bf16[3,1,128,3072]{3,2,1,0:T(8,128)(2,1)}, u32[]{:S(2)}, u32[]{:S(2)}) collective-permute-start(bf16[3,1,128,3072]{3,2,1,0:T(8,128)(2,1)} %pad_maximum_fusion), channel_id=1, source_target_pairs={{1,0},{2,1},{3,2},{4,3},{5,4},{6,5},{7,6},{8,7},{9,8},{10,9},{11,1... | collective-permute-start | bytes 7077896 | tf_op jit(solution)/shard_map/ppermute | solution.py:22
  153.2 2.6 copy-start.4
  155.8 2.1 copy-start.3
  182.4 3.3 %copy-start.1 = (f32[5,128,1536]{2,1,0:T(8,128)S(1)}, f32[5,128,1536]{2,1,0:T(8,128)}, u32[]{:S(2)}) copy-start(f32[5,128,1536]{2,1,0:T(8,128)} %reshape.88) | copy-start | bytes 11796484
  186.1 4.7 %copy-start = (f32[5,128,3072]{2,1,0:T(8,128)}, f32[5,128,3072]{2,1,0:T(8,128)S(1)}, u32[]{:S(2)}) copy-start(f32[5,128,3072]{2,1,0:T(8,128)S(1)} %constant_dynamic-update-slice_fusion.2) | copy-start | bytes 23592964
  186.1 14.5 %copy-start.2 = (bf16[640,12,128]{0,2,1:T(8,128)(2,1)S(1)}, bf16[640,12,128]{0,2,1:T(8,128)(2,1)}, u32[]{:S(2)}) copy-start(bf16[640,12,128]{0,2,1:T(8,128)(2,1)} %copy.68) | copy-start | bytes 5898244
  190.8 71.5 %collective-permute-start.4 = (f32[128,3072]{1,0:T(8,128)}, f32[128,3072]{1,0:T(8,128)}, u32[]{:S(2)}, u32[]{:S(2)}) collective-permute-start(f32[128,3072]{1,0:T(8,128)} %get-tuple-element.20), channel_id=1, source_target_pairs={{1,0},{2,1},{3,2},{4,3},{5,4},{6,5},{7,6},{8,7},{9,8},{10,9},{11,1... | collective-permute-start | bytes 4718600 | tf_op jit(solution)/shard_map/ppermute | solution.py:30
  193.7 71.0 %collective-permute-start.7 = (f32[128,3072]{1,0:T(8,128)}, f32[128,3072]{1,0:T(8,128)}, u32[]{:S(2)}, u32[]{:S(2)}) collective-permute-start(f32[128,3072]{1,0:T(8,128)} %get-tuple-element.21), channel_id=1, source_target_pairs={{0,16},{16,32},{32,48},{48,64},{64,80},{80,96},{96,112},{112,128},... | collective-permute-start | bytes 4718600 | tf_op jit(solution)/shard_map/ppermute | solution.py:30
  196.6 69.0 %collective-permute-start.6 = (f32[128,3072]{1,0:T(8,128)}, f32[128,3072]{1,0:T(8,128)}, u32[]{:S(2)}, u32[]{:S(2)}) collective-permute-start(f32[128,3072]{1,0:T(8,128)} %get-tuple-element.22), channel_id=1, source_target_pairs={{16,0},{32,16},{48,32},{64,48},{80,64},{96,80},{112,96},{128,112},... | collective-permute-start | bytes 4718600 | tf_op jit(solution)/shard_map/ppermute | solution.py:30
  198.5 82.9 %collective-permute-start.5 = (f32[128,3072]{1,0:T(8,128)S(1)}, f32[128,3072]{1,0:T(8,128)}, u32[]{:S(2)}, u32[]{:S(2)}) collective-permute-start(f32[128,3072]{1,0:T(8,128)S(1)} %get-tuple-element.23), channel_id=1, source_target_pairs={{0,1},{1,2},{2,3},{3,4},{4,5},{5,6},{6,7},{7,8},{8,9},{9,10},{10,1... | collective-permute-start | bytes 4718600 | tf_op jit(solution)/shard_map/ppermute | solution.py:30
where the time goes:
time: 289 us; the launch traced here: 286 us
  waiting for transfers between devices  182 us (63%)
  local copies, waits for them, and re-layouts  58.2 us (20%)
  starting transfers between devices  25.3 us (9%)
  matrix products  11.6 us (4%)
  other arithmetic  8.38 us (3%)
    ppermute x2, waiting for transfers between devices, with_halo(): lax.ppermute(lax.slice_in_dim(block, block.shape[dim] - width, None, axis...  96.1 us
    ppermute x4, waiting for transfers between devices, passed_along(): lax.ppermute(value, axis, [(source, source + steps) for source in range(f...  77.5 us
    another operation x4, local copies, waits for them, and re-layouts, split_heads(): return token_rows.reshape(token_rows.shape[0], HEADS, HEAD_DIM)  14.2 us
    unnamed x23, local copies, waits for them, and re-layouts  14.1 us
    ppermute x4, starting transfers between devices, passed_along(): lax.ppermute(value, axis, [(source, source + steps) for source in range(f...  9.78 us
    ppermute x2, starting transfers between devices, with_halo(): lax.ppermute(lax.slice_in_dim(block, block.shape[dim] - width, None, axis...  9.7 us
    ppermute x2, waiting for transfers between devices, with_halo(): lax.ppermute(lax.slice_in_dim(block, 0, width, axis=dim), axis, backward)  8.27 us
    transpose x1, local copies, waits for them, and re-layouts, body(): jnp.einsum('hqk,qhd->khd', prob_low, grad_heads, preferred_element_type=j...  6.88 us
  transfers between devices with their start and end apart: 8, of which 8 were waited for; matrix products, arithmetic and copies ran while one was open for 2% of the time, Pallas kernels for 0%

commit v1 on v0

v1 whole, which is shorter than its diff:
```python
import functools
import math

import jax
import jax.numpy as jnp
from jax import lax
from jax.experimental import pallas as pl
from jax.experimental.pallas import tpu as pltpu
from jax.sharding import PartitionSpec as P

MESH = pl.DeviceIdType.MESH
HEAD_DIM = 128
TILE_TOKENS = 64
BLOCK = 128
MASKED = -1e30
SCALE = HEAD_DIM ** (-0.5)
SCALE_LOG2E = SCALE * math.log2(math.e)

OWN, C, Y, X, F = range(5)
GROUP = 2
LAG_PHASE1, LAG_COMBINE, LAG_PHASE2, LAG_XRET, LAG_FINAL = 1, 2, 3, 4, 5


def kernel(
    slabs,
    bands,
    chunks,
    q_hbm,
    k_hbm,
    v_hbm,
    g_hbm,
    window,
    dq_out,
    dk_out,
    dv_out,
    k_ref,
    v_ref,
    qd,
    weight,
    gprob,
    bias_out,
    bias_in,
    st_own,
    st_out,
    st_in,
    fin_own,
    fin_out,
    fin_in,
    dq_own,
    dq_send,
    dq_in,
    load_sem,
    bias_ssem,
    bias_rsem,
    fwd_ssem,
    fwd_rsem,
    st_ssem,
    st_rsem,
    fin_ssem,
    fin_rsem,
    dq_ssem,
    dq_rsem,
):
    t = lax.axis_index("tm")
    b = lax.axis_index("space")
    todd = lax.rem(t, 2)
    bodd = lax.rem(b, 2)
    tstep = 2 * todd - 1
    bstep = 1 - 2 * bodd
    t_c = t - tstep
    t_y = t + tstep
    b_x = b + bstep
    b_f = b - bstep
    b_zout = b + 2 * bstep
    b_zin = b - 2 * bstep
    has_y = (t_y >= 0) & (t_y < slabs)
    has_f = (b_f >= 0) & (b_f < bands)
    has_zout = (b_zout >= 0) & (b_zout < bands)
    bent = (t == slabs // 2 - 1) | (t == slabs // 2)
    straight = has_y & jnp.logical_not(bent)
    b_y = jnp.where(bent, b_x, b)

    partner = {C: (t_c, b), Y: (t_y, b), X: (t, b_x), F: (t, b_f)}
    present = {C: None, Y: has_y, X: None, F: has_f}
    bulk_y = (t_y, b_y)
    zout, zin = (t, b_zout), (t, b_zin)

    def guarded(condition, action):
        if condition is None:
            action()
        else:
            pl.when(condition)(action)

    def load_chunk(c, which):
        src = (q_hbm, g_hbm)[which]
        cols = pl.ds(pl.multiple_of(c * GROUP * HEAD_DIM, GROUP * HEAD_DIM), GROUP * HEAD_DIM)
        return pltpu.make_async_copy(
            src.at[0, 0, :, cols], qd.at[OWN, c, which], load_sem.at[which, c]
        )

    k_load = pltpu.make_async_copy(k_hbm.at[0, 0], k_ref, load_sem.at[2, 0])
    v_load = pltpu.make_async_copy(v_hbm.at[0, 0], v_ref, load_sem.at[2, 1])

    @pl.loop(0, chunks)
    def _(c):
        load_chunk(c, 0).start()
        load_chunk(c, 1).start()

    k_load.start()
    v_load.start()

    barrier = pltpu.get_barrier_semaphore()

    def greet(device):
        pl.semaphore_signal(barrier, inc=1, device_id=device, device_id_type=MESH)

    for n in (C, Y, X, F):
        guarded(present[n], functools.partial(greet, partner[n]))
    guarded(bent, functools.partial(greet, bulk_y))
    guarded(has_zout, functools.partial(greet, zout))
    guarded(has_f, functools.partial(greet, zin))

    lane_tile = lax.broadcasted_iota(jnp.int32, (1, BLOCK), 1) // TILE_TOKENS
    dirs = {
        OWN: (0, 0),
        C: (-tstep, 0),
        Y: (tstep, 0),
        X: (0, bstep),
        F: (0, -bstep),
    }
    for n in (OWN, C, Y, X, F):
        dt, dr = dirs[n]
        for key_tile in range(2):
            row = None
            for query_tile in range(2):
                dc = key_tile - query_tile
                if n == OWN and dc == 0:
                    value = jnp.float32(0.0)
                else:
                    code = 9 * (dt + 1) + 3 * (dr + 1) + dc + 1
                    listed = window[0, 0, query_tile, code]
                    value = jnp.where(listed == 1, 0.0, MASKED).astype(jnp.float32)
                part = jnp.full((1, BLOCK), value, jnp.float32)
                row = part if row is None else jnp.where(lane_tile == 0, row, part)
            if n == OWN:
                bias_in[OWN, key_tile] = row
            else:
                bias_out[n, key_tile] = row

    def blank(n):
        bias_in[n] = jnp.zeros_like(bias_in[n])

        @pl.loop(0, chunks)
        def _(c):
            qd[n, c] = jnp.zeros(qd.shape[2:], qd.dtype)
            for g in range(GROUP):
                st_in[n, c, 3 * g] = jnp.full((1, BLOCK), MASKED, jnp.float32)
                st_in[n, c, 3 * g + 1] = jnp.zeros((1, BLOCK), jnp.float32)
                st_in[n, c, 3 * g + 2] = jnp.zeros((1, BLOCK), jnp.float32)
                fin_in[n, c, 2 * g] = jnp.zeros((1, BLOCK), jnp.float32)
                fin_in[n, c, 2 * g + 1] = jnp.zeros((1, BLOCK), jnp.float32)
            if n != F:
                dq_in[n, c] = jnp.zeros(dq_in.shape[2:], dq_in.dtype)

    pl.when(jnp.logical_not(has_y))(functools.partial(blank, Y))
    pl.when(jnp.logical_not(has_f))(functools.partial(blank, F))

    @pl.when(jnp.logical_not(has_zout))
    def _():
        @pl.loop(0, chunks)
        def _(c):
            dq_in[F, c] = jnp.zeros(dq_in.shape[2:], dq_in.dtype)

    count = 2 + 2 * has_f.astype(jnp.int32) + has_y.astype(jnp.int32)
    count = count + bent.astype(jnp.int32) + has_zout.astype(jnp.int32)
    pl.semaphore_wait(barrier, count)

    def remote(src, dst, send, recv, device):
        return pltpu.make_async_remote_copy(
            src_ref=src,
            dst_ref=dst,
            send_sem=send,
            recv_sem=recv,
            device_id=device,
            device_id_type=MESH,
        )

    def bias_copy(n):
        return remote(
            bias_out.at[n], bias_in.at[n], bias_ssem.at[n], bias_rsem.at[n], partner[n]
        )

    def forward(n, c):
        return remote(
            qd.at[OWN, c], qd.at[n, c], fwd_ssem.at[n, c], fwd_rsem.at[n, c], partner[n]
        )

    def bent_forward(c):
        return remote(qd.at[X, c], qd.at[Y, c], fwd_ssem.at[Y, c], fwd_rsem.at[Y, c], bulk_y)

    def relay(c):
        return remote(qd.at[X, c], qd.at[F, c], fwd_ssem.at[F, c], fwd_rsem.at[F, c], zout)

    def st_copy(n, c):
        return remote(
            st_out.at[n, c], st_in.at[n, c], st_ssem.at[n, c], st_rsem.at[n, c], partner[n]
        )

    def fin_copy(n, c):
        return remote(
            fin_out.at[n, c], fin_in.at[n, c], fin_ssem.at[n, c], fin_rsem.at[n, c], partner[n]
        )

    def dq_copy(n, c):
        device = {C: partner[C], Y: bulk_y, X: partner[X], F: zin}[n]
        return remote(
            dq_send.at[n, c], dq_in.at[n, c], dq_ssem.at[n, c], dq_rsem.at[n, c], device
        )

    for n in (X, F, C, Y):
        guarded(present[n], lambda n=n: bias_copy(n).start())

    @pl.loop(0, chunks)
    def _(c):
        load_chunk(c, 0).wait()
        load_chunk(c, 1).wait()
        forward(X, c).start()
        forward(C, c).start()

        @pl.when(straight)
        def _():
            forward(Y, c).start()

    k_load.wait()
    v_load.wait()
    for n in (X, F, C, Y):
        guarded(present[n], lambda n=n: bias_copy(n).wait_recv())

    def head_cols(c, g):
        return pl.ds(pl.multiple_of((c * GROUP + g) * HEAD_DIM, HEAD_DIM), HEAD_DIM)

    def nearby(c, which, g):
        cols = slice(g * HEAD_DIM, (g + 1) * HEAD_DIM)
        return jnp.concatenate([qd[n, c, which, :, cols] for n in range(5)], axis=0)

    def stage_relay(c):
        forward(X, c).wait_recv()

        @pl.when(has_zout)
        def _():
            relay(c).start()

        @pl.when(bent)
        def _():
            bent_forward(c).start()

    def stage_phase1(c):
        forward(C, c).wait_recv()

        @pl.when(has_y)
        def _():
            forward(Y, c).wait_recv()

        @pl.when(has_f)
        def _():
            relay(c).wait_recv()

        masks = jnp.concatenate(
            [
                jnp.concatenate([bias_in[n, key_tile] for n in range(5)], axis=1)
                for key_tile in range(2)
            ],
            axis=0,
        )
        for g in range(GROUP):
            keys = k_ref[:, head_cols(c, g)]
            values = v_ref[:, head_cols(c, g)]
            contract = (((1,), (1,)), ((), ()))
            scores = lax.dot_general(
                keys, nearby(c, 0, g), contract, preferred_element_type=jnp.float32
            )
            scores = jnp.concatenate(
                [scores[:TILE_TOKENS] + masks[0:1], scores[TILE_TOKENS:] + masks[1:2]], axis=0
            )
            top = jnp.max(scores, axis=0, keepdims=True)
            powers = jnp.exp2((scores - top) * SCALE_LOG2E)
            weight[c, g] = powers
            total = jnp.sum(powers, axis=0, keepdims=True)
            grad_probs = lax.dot_general(
                values, nearby(c, 1, g), contract, preferred_element_type=jnp.float32
            )
            gprob[c, g] = grad_probs
            mixed = jnp.sum(powers * grad_probs, axis=0, keepdims=True)
            for n in range(5):
                span = slice(n * BLOCK, (n + 1) * BLOCK)
                for at, row in enumerate((top, total, mixed)):
                    if n == OWN:
                        st_own[c, 3 * g + at] = row[:, span]
                    else:
                        st_out[n, c, 3 * g + at] = row[:, span]
        for n in (F, X, Y, C):
            guarded(present[n], lambda n=n: st_copy(n, c).start())

    def stage_combine(c):
        for n in (C, Y, X, F):
            guarded(present[n], lambda n=n: st_copy(n, c).wait_recv())
        for g in range(GROUP):
            tops = [st_own[c, 3 * g]] + [st_in[n, c, 3 * g] for n in (C, Y, X, F)]
            totals = [st_own[c, 3 * g + 1]] + [st_in[n, c, 3 * g + 1] for n in (C, Y, X, F)]
            mixes = [st_own[c, 3 * g + 2]] + [st_in[n, c, 3 * g + 2] for n in (C, Y, X, F)]
            top = functools.reduce(jnp.maximum, tops)
            shares = [jnp.exp2((each - top) * SCALE_LOG2E) for each in tops]
            total = sum(share * each for share, each in zip(shares, totals))
            inverse = 1.0 / total
            delta = sum(share * each for share, each in zip(shares, mixes)) * inverse
            fin_own[c, 2 * g] = shares[OWN] * inverse
            fin_own[c, 2 * g + 1] = delta
            for n in (C, Y, X, F):
                fin_out[n, c, 2 * g] = shares[n] * inverse
                fin_out[n, c, 2 * g + 1] = delta
        for n in (F, X, Y, C):
            guarded(present[n], lambda n=n: fin_copy(n, c).start())

    def stage_phase2(c):
        for n in (C, Y, X, F):
            guarded(present[n], lambda n=n: fin_copy(n, c).wait_recv())
        for g in range(GROUP):
            cols = head_cols(c, g)
            factor = jnp.concatenate(
                [fin_own[c, 2 * g]] + [fin_in[n, c, 2 * g] for n in (C, Y, X, F)], axis=1
            )
            delta = jnp.concatenate(
                [fin_own[c, 2 * g + 1]] + [fin_in[n, c, 2 * g + 1] for n in (C, Y, X, F)], axis=1
            )
            powers = weight[c, g]
            probs = powers * factor
            grad_scores = (probs * ((gprob[c, g] - delta) * SCALE)).astype(jnp.bfloat16)
            plain = (((1,), (0,)), ((), ()))
            dv_out[0, 0, :, cols] = lax.dot_general(
                probs.astype(jnp.bfloat16),
                nearby(c, 1, g),
                plain,
                preferred_element_type=jnp.float32,
            ).astype(jnp.bfloat16)
            dk_out[0, 0, :, cols] = lax.dot_general(
                grad_scores, nearby(c, 0, g), plain, preferred_element_type=jnp.float32
            ).astype(jnp.bfloat16)
            turned = lax.dot_general(
                k_ref[:, cols],
                grad_scores,
                (((0,), (0,)), ((), ())),
                preferred_element_type=jnp.float32,
            )
            dq_own[0, c, g] = turned[:, :BLOCK]
            dq_own[1, c, g] = turned[:, X * BLOCK : (X + 1) * BLOCK]
            for n in (C, Y, F):
                dq_send[n, c, g] = turned[:, n * BLOCK : (n + 1) * BLOCK].astype(jnp.bfloat16)
        guarded(has_f, lambda: dq_copy(F, c).start())
        guarded(has_y, lambda: dq_copy(Y, c).start())
        dq_copy(C, c).start()

    def stage_xret(c):
        guarded(has_zout, lambda: dq_copy(F, c).wait_recv())

        @pl.when(bent)
        def _():
            dq_copy(Y, c).wait_recv()
            for g in range(GROUP):
                dq_own[1, c, g] = dq_own[1, c, g] + dq_in[Y, c, g].astype(jnp.float32)
                dq_in[Y, c, g] = jnp.zeros(dq_in.shape[3:], dq_in.dtype)

        for g in range(GROUP):
            dq_send[X, c, g] = (dq_own[1, c, g] + dq_in[F, c, g].astype(jnp.float32)).astype(
                jnp.bfloat16
            )
        dq_copy(X, c).start()

    def stage_final(c):
        dq_copy(C, c).wait_recv()
        guarded(straight, lambda: dq_copy(Y, c).wait_recv())
        dq_copy(X, c).wait_recv()
        for g in range(GROUP):
            total = dq_own[0, c, g]
            for n in (C, Y, X):
                total = total + dq_in[n, c, g].astype(jnp.float32)
            dq_out[0, 0, :, head_cols(c, g)] = total.T.astype(jnp.bfloat16)

    stages = (
        (0, stage_relay),
        (LAG_PHASE1, stage_phase1),
        (LAG_COMBINE, stage_combine),
        (LAG_PHASE2, stage_phase2),
        (LAG_XRET, stage_xret),
        (LAG_FINAL, stage_final),
    )

    @pl.loop(0, chunks + LAG_FINAL)
    def _(tick):
        for lag, stage in stages:

            @pl.when((tick >= lag) & (tick < chunks + lag))
            def _(lag=lag, stage=stage):
                stage(tick - lag)

    for n in (X, F, C, Y):
        guarded(present[n], lambda n=n: bias_copy(n).wait_send())

    @pl.loop(0, chunks)
    def _(c):
        forward(X, c).wait_send()
        forward(C, c).wait_send()
        guarded(has_y, lambda: bent_forward(c).wait_send())
        guarded(has_zout, lambda: relay(c).wait_send())
        for n in (C, Y, X, F):
            guarded(present[n], lambda n=n: st_copy(n, c).wait_send())
            guarded(present[n], lambda n=n: fin_copy(n, c).wait_send())
            guarded(present[n], lambda n=n: dq_copy(n, c).wait_send())


def body(slabs, bands, queries, key_states, value_states, grad_out, window):
    features = queries.shape[3]
    heads = features // HEAD_DIM
    chunks = heads // GROUP
    wide = GROUP * HEAD_DIM
    f32, bf16 = jnp.float32, jnp.bfloat16
    dma = pltpu.SemaphoreType.DMA
    out = jax.ShapeDtypeStruct(queries.shape, bf16)
    anywhere = pl.BlockSpec(memory_space=pl.ANY)
    vmem = pl.BlockSpec(memory_space=pltpu.VMEM)
    macs = heads * 5 * 5 * BLOCK * BLOCK * HEAD_DIM
    return pl.pallas_call(
        functools.partial(kernel, slabs, bands, chunks),
        out_shape=(out, out, out),
        in_specs=[anywhere] * 4 + [pl.BlockSpec(memory_space=pltpu.SMEM)],
        out_specs=(vmem, vmem, vmem),
        scratch_shapes=[
            pltpu.VMEM((BLOCK, features), bf16),
            pltpu.VMEM((BLOCK, features), bf16),
            pltpu.VMEM((5, chunks, 2, BLOCK, wide), bf16),
            pltpu.VMEM((chunks, GROUP, BLOCK, 5 * BLOCK), f32),
            pltpu.VMEM((chunks, GROUP, BLOCK, 5 * BLOCK), f32),
            pltpu.VMEM((5, 2, 1, BLOCK), f32),
            pltpu.VMEM((5, 2, 1, BLOCK), f32),
            pltpu.VMEM((chunks, 3 * GROUP, 1, BLOCK), f32),
            pltpu.VMEM((5, chunks, 3 * GROUP, 1, BLOCK), f32),
            pltpu.VMEM((5, chunks, 3 * GROUP, 1, BLOCK), f32),
            pltpu.VMEM((chunks, 2 * GROUP, 1, BLOCK), f32),
            pltpu.VMEM((5, chunks, 2 * GROUP, 1, BLOCK), f32),
            pltpu.VMEM((5, chunks, 2 * GROUP, 1, BLOCK), f32),
            pltpu.VMEM((2, chunks, GROUP, HEAD_DIM, BLOCK), f32),
            pltpu.VMEM((5, chunks, GROUP, HEAD_DIM, BLOCK), bf16),
            pltpu.VMEM((5, chunks, GROUP, HEAD_DIM, BLOCK), bf16),
            dma((3, chunks)),
            dma((5,)),
            dma((5,)),
            dma((5, chunks)),
            dma((5, chunks)),
            dma((5, chunks)),
            dma((5, chunks)),
            dma((5, chunks)),
            dma((5, chunks)),
            dma((5, chunks)),
            dma((5, chunks)),
        ],
        compiler_params=pltpu.CompilerParams(
            collective_id=0, has_side_effects=True, vmem_limit_bytes=40 << 20
        ),
        cost_estimate=pl.CostEstimate(
            flops=2 * macs,
            bytes_accessed=7 * BLOCK * features * 2,
            transcendentals=heads * 5 * BLOCK * BLOCK,
        ),
    )(queries, key_states, value_states, grad_out, window)


def solution(mesh):
    spec = P("tm", "space", None, None)
    return jax.shard_map(
        functools.partial(body, mesh.shape["tm"], mesh.shape["space"]),
        mesh=mesh,
        in_specs=(spec,) * 5,
        out_specs=(spec,) * 3,
        check_vma=False,
    )
```

time: 289 us -> 66.5 us (0.23)
  the two profiles are of different devices: /device:TPU:121 before, /device:TPU:36 now
where the time goes in v1:
time: 66.5 us; the launch traced here: 66.2 us
  Pallas kernels  58.7 us (88%)
  local copies, waits for them, and re-layouts  6.89 us (10%)
    pallas_call x1, Pallas kernels, body(): pl.pallas_call(functools.partial(kernel, slabs, bands, chunks), out_shape...  58.7 us
    unnamed x13, local copies, waits for them, and re-layouts  6.89 us

profile of v1, /device:TPU:36, one launch (start us, length us, event | category | flops | bytes accessed | tf_op | source)
XLA Modules:
  0.0 66.2 jit_solution(11612135916320245470)
XLA Ops:
  0.6 0.0 copy-start
  0.6 1.0 %copy-done = bf16[1,1,128,1536]{3,2,1,0:T(8,128)(2,1)S(1)} copy-done((bf16[1,1,128,1536]{3,2,1,0:T(8,128)(2,1)S(1)}, bf16[1,1,128,1536]{3,2,1,0:T(8,128)(2,1)}, u32[]{:S(2)}) %copy-start) | copy-done | bytes 393240
  1.6 0.0 copy-start.1
  1.6 1.0 %copy-done.1 = bf16[1,1,128,1536]{3,2,1,0:T(8,128)(2,1)S(1)} copy-done((bf16[1,1,128,1536]{3,2,1,0:T(8,128)(2,1)S(1)}, bf16[1,1,128,1536]{3,2,1,0:T(8,128)(2,1)}, u32[]{:S(2)}) %copy-start.1) | copy-done | bytes 393240
  2.6 0.0 copy-start.2
  2.6 1.0 %copy-done.2 = bf16[1,1,128,1536]{3,2,1,0:T(8,128)(2,1)S(1)} copy-done((bf16[1,1,128,1536]{3,2,1,0:T(8,128)(2,1)S(1)}, bf16[1,1,128,1536]{3,2,1,0:T(8,128)(2,1)}, u32[]{:S(2)}) %copy-start.2) | copy-done | bytes 393240
  3.6 0.0 copy-start.3
  3.6 1.0 %copy-done.3 = bf16[1,1,128,1536]{3,2,1,0:T(8,128)(2,1)S(1)} copy-done((bf16[1,1,128,1536]{3,2,1,0:T(8,128)(2,1)S(1)}, bf16[1,1,128,1536]{3,2,1,0:T(8,128)(2,1)}, u32[]{:S(2)}) %copy-start.3) | copy-done | bytes 393240
  4.6 0.0 copy-start.4
  4.6 0.7 %copy-done.4 = s32[1,1,2,27]{3,2,1,0:T(2,128)S(1)} copy-done((s32[1,1,2,27]{3,2,1,0:T(2,128)S(1)}, s32[1,1,2,27]{3,2,1,0:T(2,128)}, u32[]{:S(2)}) %copy-start.4) | copy-done | bytes 240
  5.3 58.7 %shard_map.76 = (bf16[1,1,128,1536]{3,2,1,0:T(8,128)(2,1)S(1)}, bf16[1,1,128,1536]{3,2,1,0:T(8,128)(2,1)S(1)}, bf16[1,1,128,1536]{3,2,1,0:T(8,128)(2,1)S(1)}) custom-call(bf16[1,1,128,1536]{3,2,1,0:T(8,128)(2,1)S(1)} %copy-done, bf16[1,1,128,1536]{3,2,1,0:T(8,128)(2,1)S(1)} %copy-done.1, bf16[1,1,128,1536]{3,2,1,0:T(8,128)(2,1)S(1)} %copy-done.2, ...), custom_call_target="tpu_custom_call" | custom-call | flops 1258291200 | bytes 2752512 | tf_op jit(solution)/shard_map/pallas_call | solution.py:431
  64.0 0.7 %copy.11 = bf16[1,1,128,1536]{3,2,1,0:T(8,128)(2,1)} copy(bf16[1,1,128,1536]{3,2,1,0:T(8,128)(2,1)S(1)} %get-tuple-element.6) | data formatting | bytes 786432
  64.7 0.7 %copy.12 = bf16[1,1,128,1536]{3,2,1,0:T(8,128)(2,1)} copy(bf16[1,1,128,1536]{3,2,1,0:T(8,128)(2,1)S(1)} %get-tuple-element.7) | data formatting | bytes 786432
  65.5 0.7 %copy.13 = bf16[1,1,128,1536]{3,2,1,0:T(8,128)(2,1)} copy(bf16[1,1,128,1536]{3,2,1,0:T(8,128)(2,1)S(1)} %get-tuple-element.8) | data formatting | bytes 786432
Async XLA Ops:
  0.6 1.0 %copy-start = (bf16[1,1,128,1536]{3,2,1,0:T(8,128)(2,1)S(1)}, bf16[1,1,128,1536]{3,2,1,0:T(8,128)(2,1)}, u32[]{:S(2)}) copy-start(bf16[1,1,128,1536]{3,2,1,0:T(8,128)(2,1)} %q_hbm.1) | copy-start | bytes 1179652
  1.6 1.0 %copy-start.1 = (bf16[1,1,128,1536]{3,2,1,0:T(8,128)(2,1)S(1)}, bf16[1,1,128,1536]{3,2,1,0:T(8,128)(2,1)}, u32[]{:S(2)}) copy-start(bf16[1,1,128,1536]{3,2,1,0:T(8,128)(2,1)} %k_hbm.1) | copy-start | bytes 1179652
  2.6 1.0 %copy-start.2 = (bf16[1,1,128,1536]{3,2,1,0:T(8,128)(2,1)S(1)}, bf16[1,1,128,1536]{3,2,1,0:T(8,128)(2,1)}, u32[]{:S(2)}) copy-start(bf16[1,1,128,1536]{3,2,1,0:T(8,128)(2,1)} %v_hbm.1) | copy-start | bytes 1179652
  3.6 1.0 %copy-start.3 = (bf16[1,1,128,1536]{3,2,1,0:T(8,128)(2,1)S(1)}, bf16[1,1,128,1536]{3,2,1,0:T(8,128)(2,1)}, u32[]{:S(2)}) copy-start(bf16[1,1,128,1536]{3,2,1,0:T(8,128)(2,1)} %g_hbm.1) | copy-start | bytes 1179652
  4.6 0.7 %copy-start.4 = (s32[1,1,2,27]{3,2,1,0:T(2,128)S(1)}, s32[1,1,2,27]{3,2,1,0:T(2,128)}, u32[]{:S(2)}) copy-start(s32[1,1,2,27]{3,2,1,0:T(2,128)} %window.1) | copy-start | bytes 652

commit v2 on v1

v2 whole, which is shorter than its diff:
```python
import functools
import math

import jax
import jax.numpy as jnp
from jax import lax
from jax.experimental import pallas as pl
from jax.experimental.pallas import tpu as pltpu
from jax.sharding import PartitionSpec as P

MESH = pl.DeviceIdType.MESH
HEAD_DIM = 128
TILE_TOKENS = 64
BLOCK = 128
MASKED = -1e30
SCALE = HEAD_DIM ** (-0.5)
SCALE_LOG2E = SCALE * math.log2(math.e)

OWN, C, Y, X, F = range(5)
RETURNED = 6
AHEAD = 3
LAG_ARRIVED, LAG_COMBINE, LAG_PHASE2, LAG_XRET, LAG_FINAL = 3, 6, 9, 12, 15


def kernel(
    slabs,
    bands,
    heads,
    q_hbm,
    k_hbm,
    v_hbm,
    g_hbm,
    window,
    dq_out,
    dk_out,
    dv_out,
    k_ref,
    v_ref,
    fw,
    weight,
    gprob,
    bias_out,
    bias_in,
    st_own,
    st_out,
    st_in,
    fin_own,
    fin_out,
    fin_in,
    row_own,
    row_in,
    dq_own,
    dq_send,
    dq_in,
    load_sem,
    bias_ssem,
    bias_rsem,
    fwd_ssem,
    fwd_rsem,
    st_ssem,
    st_rsem,
    fin_ssem,
    fin_rsem,
    row_ssem,
    row_rsem,
    dq_ssem,
    dq_rsem,
):
    local = heads - RETURNED
    messages = RETURNED + 2 * local
    t = lax.axis_index("tm")
    b = lax.axis_index("space")
    todd = lax.rem(t, 2)
    bodd = lax.rem(b, 2)
    tstep = 2 * todd - 1
    bstep = 1 - 2 * bodd
    t_c = t - tstep
    t_y = t + tstep
    b_x = b + bstep
    b_f = b - bstep
    b_zout = b + 2 * bstep
    b_zin = b - 2 * bstep
    has_y = (t_y >= 0) & (t_y < slabs)
    has_f = (b_f >= 0) & (b_f < bands)
    has_zout = (b_zout >= 0) & (b_zout < bands)
    bent = (t == slabs // 2 - 1) | (t == slabs // 2)
    straight = has_y & jnp.logical_not(bent)
    b_y = jnp.where(bent, b_x, b)

    partner = {C: (t_c, b), Y: (t_y, b), X: (t, b_x), F: (t, b_f)}
    present = {C: None, Y: has_y, X: None, F: has_f}
    bulk_y = (t_y, b_y)
    zout, zin = (t, b_zout), (t, b_zin)

    def guarded(condition, action):
        if condition is None:
            action()
        else:
            pl.when(condition)(action)

    def head_cols(h):
        return pl.ds(pl.multiple_of(h * HEAD_DIM, HEAD_DIM), HEAD_DIM)

    def load(m, h, src, piece):
        return pltpu.make_async_copy(
            src.at[0, 0, :, head_cols(h)], fw.at[OWN, m, piece], load_sem.at[piece, m]
        )

    def each_load(m, act):
        @pl.when(m < RETURNED)
        def _():
            act(load(m, m, q_hbm, 0))
            act(load(m, m, g_hbm, 1))

        @pl.when((m >= RETURNED) & (m < heads))
        def _():
            act(load(m, m, k_hbm, 0))
            act(load(m, m, v_hbm, 1))

        @pl.when(m >= heads)
        def _():
            act(load(m, m - local, q_hbm, 0))
            act(load(m, m - local, g_hbm, 1))

    k_load = pltpu.make_async_copy(k_hbm.at[0, 0], k_ref, load_sem.at[2, 0])
    v_load = pltpu.make_async_copy(v_hbm.at[0, 0], v_ref, load_sem.at[2, 1])

    @pl.loop(0, messages)
    def _(m):
        each_load(m, lambda copy: copy.start())

    k_load.start()
    v_load.start()

    barrier = pltpu.get_barrier_semaphore()

    def greet(device):
        pl.semaphore_signal(barrier, inc=1, device_id=device, device_id_type=MESH)

    for n in (C, Y, X, F):
        guarded(present[n], functools.partial(greet, partner[n]))
    guarded(bent, functools.partial(greet, bulk_y))
    guarded(has_zout, functools.partial(greet, zout))
    guarded(has_f, functools.partial(greet, zin))

    lane_tile = lax.broadcasted_iota(jnp.int32, (1, BLOCK), 1) // TILE_TOKENS
    dirs = {
        OWN: (0, 0),
        C: (-tstep, 0),
        Y: (tstep, 0),
        X: (0, bstep),
        F: (0, -bstep),
    }
    for n in (OWN, C, Y, X, F):
        dt, dr = dirs[n]
        for key_tile in range(2):
            row = None
            for query_tile in range(2):
                dc = key_tile - query_tile
                if n == OWN and dc == 0:
                    value = jnp.float32(0.0)
                else:
                    code = 9 * (dt + 1) + 3 * (dr + 1) + dc + 1
                    listed = window[0, 0, query_tile, code]
                    shown = listed == 1
                    if n != OWN and present[n] is not None:
                        shown = shown & present[n]
                    value = jnp.where(shown, 0.0, MASKED).astype(jnp.float32)
                part = jnp.full((1, BLOCK), value, jnp.float32)
                row = part if row is None else jnp.where(lane_tile == 0, row, part)
            if n == OWN:
                bias_in[OWN, key_tile] = row
            else:
                bias_out[n, key_tile] = row

    def blank(n):
        bias_in[n] = jnp.zeros_like(bias_in[n])

        @pl.loop(0, messages)
        def _(m):
            fw[n, m] = jnp.zeros(fw.shape[2:], fw.dtype)

        zero_row = jnp.zeros((1, BLOCK), jnp.float32)

        @pl.loop(0, RETURNED)
        def _(h):
            st_in[n, h, 0] = jnp.full((1, BLOCK), MASKED, jnp.float32)
            st_in[n, h, 1] = zero_row
            st_in[n, h, 2] = zero_row
            fin_in[n, h, 0] = zero_row
            fin_in[n, h, 1] = zero_row
            if n != F:
                dq_in[n, h] = jnp.zeros(dq_in.shape[2:], dq_in.dtype)

        @pl.loop(0, local)
        def _(j):
            for at in range(3):
                row_in[n, j, at] = zero_row

    pl.when(jnp.logical_not(has_y))(functools.partial(blank, Y))
    pl.when(jnp.logical_not(has_f))(functools.partial(blank, F))

    @pl.when(jnp.logical_not(has_zout))
    def _():
        @pl.loop(0, RETURNED)
        def _(h):
            dq_in[F, h] = jnp.zeros(dq_in.shape[2:], dq_in.dtype)

    count = 2 + 2 * has_f.astype(jnp.int32) + has_y.astype(jnp.int32)
    count = count + bent.astype(jnp.int32) + has_zout.astype(jnp.int32)
    pl.semaphore_wait(barrier, count)

    def remote(src, dst, send, recv, device):
        return pltpu.make_async_remote_copy(
            src_ref=src,
            dst_ref=dst,
            send_sem=send,
            recv_sem=recv,
            device_id=device,
            device_id_type=MESH,
        )

    def bias_copy(n):
        return remote(
            bias_out.at[n], bias_in.at[n], bias_ssem.at[n], bias_rsem.at[n], partner[n]
        )

    def forward(n, c):
        return remote(
            fw.at[OWN, c], fw.at[n, c], fwd_ssem.at[n, c], fwd_rsem.at[n, c], partner[n]
        )

    def bent_forward(c):
        return remote(fw.at[X, c], fw.at[Y, c], fwd_ssem.at[Y, c], fwd_rsem.at[Y, c], bulk_y)

    def relay(c):
        return remote(fw.at[X, c], fw.at[F, c], fwd_ssem.at[F, c], fwd_rsem.at[F, c], zout)

    def st_copy(n, c):
        return remote(
            st_out.at[n, c], st_in.at[n, c], st_ssem.at[n, c], st_rsem.at[n, c], partner[n]
        )

    def fin_copy(n, c):
        return remote(
            fin_out.at[n, c], fin_in.at[n, c], fin_ssem.at[n, c], fin_rsem.at[n, c], partner[n]
        )

    def row_copy(n, j):
        return remote(
            row_own.at[j], row_in.at[n, j], row_ssem.at[n, j], row_rsem.at[n, j], partner[n]
        )

    def dq_copy(n, c):
        device = {C: partner[C], Y: bulk_y, X: partner[X], F: zin}[n]
        return remote(
            dq_send.at[n, c], dq_in.at[n, c], dq_ssem.at[n, c], dq_rsem.at[n, c], device
        )

    for n in (X, F, C, Y):
        guarded(present[n], lambda n=n: bias_copy(n).start())

    def send_own(m):
        each_load(m, lambda copy: copy.wait())
        forward(X, m).start()
        forward(C, m).start()

        @pl.when(straight)
        def _():
            forward(Y, m).start()

    @pl.loop(0, AHEAD)
    def _(m):
        send_own(m)

    k_load.wait()
    v_load.wait()
    for n in (X, F, C, Y):
        guarded(present[n], lambda n=n: bias_copy(n).wait_recv())

    def nearby(m, piece):
        return jnp.concatenate([fw[n, m, piece] for n in range(5)], axis=0)

    def dot(a, b, a_dim, b_dim):
        return lax.dot_general(
            a, b, (((a_dim,), (b_dim,)), ((), ())), preferred_element_type=jnp.float32
        )

    def masked_for_own_keys(scores):
        masks = [
            jnp.concatenate([bias_in[n, key_tile] for n in range(5)], axis=1)
            for key_tile in range(2)
        ]
        return jnp.concatenate(
            [scores[:TILE_TOKENS] + masks[0], scores[TILE_TOKENS:] + masks[1]], axis=0
        )

    def arrived(m):
        forward(C, m).wait_recv()

        @pl.when(has_y)
        def _():
            forward(Y, m).wait_recv()

        @pl.when(has_f)
        def _():
            relay(m).wait_recv()

    def to_neighbours(copy, at):
        for n in (F, X, Y, C):
            guarded(present[n], lambda n=n: copy(n, at).start())

    def from_neighbours(copy, at):
        for n in (C, Y, X, F):
            guarded(present[n], lambda n=n: copy(n, at).wait_recv())

    def stage_relay(m):
        forward(X, m).wait_recv()

        @pl.when(has_zout)
        def _():
            relay(m).start()

        @pl.when(bent)
        def _():
            bent_forward(m).start()

        @pl.when(m + AHEAD < messages)
        def _():
            send_own(m + AHEAD)

    def stage_phase1(h):
        arrived(h)
        cols = head_cols(h)
        scores = masked_for_own_keys(dot(k_ref[:, cols], nearby(h, 0), 1, 1))
        top = jnp.max(scores, axis=0, keepdims=True)
        powers = jnp.exp2((scores - top) * SCALE_LOG2E)
        weight[h] = powers
        total = jnp.sum(powers, axis=0, keepdims=True)
        grad_probs = dot(v_ref[:, cols], nearby(h, 1), 1, 1)
        gprob[h] = grad_probs
        mixed = jnp.sum(powers * grad_probs, axis=0, keepdims=True)
        for n in range(5):
            span = slice(n * BLOCK, (n + 1) * BLOCK)
            for at, row in enumerate((top, total, mixed)):
                if n == OWN:
                    st_own[h, at] = row[:, span]
                else:
                    st_out[n, h, at] = row[:, span]
        to_neighbours(st_copy, h)

    def stage_combine(h):
        from_neighbours(st_copy, h)
        tops, totals, mixes = (
            [st_own[h, at]] + [st_in[n, h, at] for n in (C, Y, X, F)] for at in range(3)
        )
        top = functools.reduce(jnp.maximum, tops)
        shares = [jnp.exp2((each - top) * SCALE_LOG2E) for each in tops]
        inverse = 1.0 / sum(share * each for share, each in zip(shares, totals))
        delta = sum(share * each for share, each in zip(shares, mixes)) * inverse
        fin_own[h, 0] = shares[OWN] * inverse
        fin_own[h, 1] = delta
        for n in (C, Y, X, F):
            fin_out[n, h, 0] = shares[n] * inverse
            fin_out[n, h, 1] = delta
        to_neighbours(fin_copy, h)

    def own_key_grads(cols, probs, grad_probs, delta, m):
        grad_scores = (probs * ((grad_probs - delta) * SCALE)).astype(jnp.bfloat16)
        dv_out[0, 0, :, cols] = dot(probs.astype(jnp.bfloat16), nearby(m, 1), 1, 0).astype(
            jnp.bfloat16
        )
        dk_out[0, 0, :, cols] = dot(grad_scores, nearby(m, 0), 1, 0).astype(jnp.bfloat16)
        return grad_scores

    def stage_phase2(h):
        from_neighbours(fin_copy, h)
        cols = head_cols(h)
        factor, delta = (
            jnp.concatenate([fin_own[h, at]] + [fin_in[n, h, at] for n in (C, Y, X, F)], axis=1)
            for at in range(2)
        )
        grad_scores = own_key_grads(cols, weight[h] * factor, gprob[h], delta, h)
        turned = dot(k_ref[:, cols], grad_scores, 0, 0)
        dq_own[0, h] = turned[:, :BLOCK]
        dq_own[1, h] = turned[:, X * BLOCK : (X + 1) * BLOCK]
        for n in (C, Y, F):
            dq_send[n, h] = turned[:, n * BLOCK : (n + 1) * BLOCK].astype(jnp.bfloat16)
        guarded(has_f, lambda: dq_copy(F, h).start())
        guarded(has_y, lambda: dq_copy(Y, h).start())
        dq_copy(C, h).start()

    def stage_xret(h):
        guarded(has_zout, lambda: dq_copy(F, h).wait_recv())

        @pl.when(bent)
        def _():
            dq_copy(Y, h).wait_recv()
            dq_own[1, h] = dq_own[1, h] + dq_in[Y, h].astype(jnp.float32)
            dq_in[Y, h] = jnp.zeros(dq_in.shape[2:], dq_in.dtype)

        dq_send[X, h] = (dq_own[1, h] + dq_in[F, h].astype(jnp.float32)).astype(jnp.bfloat16)
        dq_copy(X, h).start()

    def stage_final(h):
        dq_copy(C, h).wait_recv()
        guarded(straight, lambda: dq_copy(Y, h).wait_recv())
        dq_copy(X, h).wait_recv()
        total = dq_own[0, h]
        for n in (C, Y, X):
            total = total + dq_in[n, h].astype(jnp.float32)
        dq_out[0, 0, :, head_cols(h)] = total.T.astype(jnp.bfloat16)

    def stage_own_rows(j):
        kv, qg = RETURNED + j, heads + j
        arrived(kv)
        keys = nearby(kv, 0)
        scores = dot(keys, fw[OWN, qg, 0], 1, 1)
        parts = []
        for n in range(5):
            for key_tile in range(2):
                mask = bias_in[OWN, key_tile] if n == OWN else bias_out[n, key_tile]
                first = n * BLOCK + key_tile * TILE_TOKENS
                parts.append(scores[first : first + TILE_TOKENS] + mask)
        scores = jnp.concatenate(parts, axis=0)
        top = jnp.max(scores, axis=0, keepdims=True)
        powers = jnp.exp2((scores - top) * SCALE_LOG2E)
        inverse = 1.0 / jnp.sum(powers, axis=0, keepdims=True)
        grad_probs = dot(nearby(kv, 1), fw[OWN, qg, 1], 1, 1)
        probs = powers * inverse
        delta = jnp.sum(probs * grad_probs, axis=0, keepdims=True)
        for at, row in enumerate((top, inverse, delta)):
            row_own[j, at] = row
        to_neighbours(row_copy, j)
        grad_scores = (probs * ((grad_probs - delta) * SCALE)).astype(jnp.bfloat16)
        dq_out[0, 0, :, head_cols(RETURNED + j)] = dot(keys, grad_scores, 0, 0).T.astype(
            jnp.bfloat16
        )

    def stage_own_keys(j):
        kv, qg = RETURNED + j, heads + j
        arrived(qg)
        from_neighbours(row_copy, j)
        top, inverse, delta = (
            jnp.concatenate([row_own[j, at]] + [row_in[n, j, at] for n in (C, Y, X, F)], axis=1)
            for at in range(3)
        )
        scores = masked_for_own_keys(dot(fw[OWN, kv, 0], nearby(qg, 0), 1, 1))
        probs = jnp.exp2((scores - top) * SCALE_LOG2E) * inverse
        grad_probs = dot(fw[OWN, kv, 1], nearby(qg, 1), 1, 1)
        own_key_grads(head_cols(RETURNED + j), probs, grad_probs, delta, qg)

    stages = (
        (0, messages, stage_relay),
        (LAG_FINAL, RETURNED, stage_final),
        (LAG_XRET, RETURNED, stage_xret),
        (LAG_PHASE2, RETURNED, stage_phase2),
        (LAG_COMBINE, RETURNED, stage_combine),
        (LAG_ARRIVED, RETURNED, stage_phase1),
        (LAG_ARRIVED + RETURNED, local, stage_own_rows),
        (LAG_ARRIVED + heads, local, stage_own_keys),
    )

    @pl.loop(0, max(messages + LAG_ARRIVED, RETURNED + LAG_FINAL))
    def _(tick):
        for lag, count, stage in stages:

            @pl.when((tick >= lag) & (tick < count + lag))
            def _(lag=lag, stage=stage):
                stage(tick - lag)

    for n in (X, F, C, Y):
        guarded(present[n], lambda n=n: bias_copy(n).wait_send())

    @pl.loop(0, messages)
    def _(m):
        forward(X, m).wait_send()
        forward(C, m).wait_send()
        guarded(has_y, lambda: bent_forward(m).wait_send())
        guarded(has_zout, lambda: relay(m).wait_send())

    for count, copies in ((RETURNED, (st_copy, fin_copy, dq_copy)), (local, (row_copy,))):

        @pl.loop(0, count)
        def _(at, copies=copies):
            for copy in copies:
                for n in (C, Y, X, F):
                    guarded(present[n], lambda n=n, copy=copy: copy(n, at).wait_send())


def store(a, b, c, a_out, b_out, c_out, sems):
    pairs = ((a, a_out), (b, b_out), (c, c_out))
    copies = [pltpu.make_async_copy(x, y, sems.at[i]) for i, (x, y) in enumerate(pairs)]
    for copy in copies:
        copy.start()
    for copy in copies:
        copy.wait()


def body(slabs, bands, queries, key_states, value_states, grad_out, window):
    features = queries.shape[3]
    heads = features // HEAD_DIM
    local = heads - RETURNED
    messages = RETURNED + 2 * local
    f32, bf16 = jnp.float32, jnp.bfloat16
    dma = pltpu.SemaphoreType.DMA
    out = jax.ShapeDtypeStruct(queries.shape, bf16)
    anywhere = pl.BlockSpec(memory_space=pl.ANY)
    vmem = pl.BlockSpec(memory_space=pltpu.VMEM)
    macs = heads * 5 * 5 * BLOCK * BLOCK * HEAD_DIM
    outs = pl.pallas_call(
        functools.partial(kernel, slabs, bands, heads),
        out_shape=(out, out, out),
        in_specs=[anywhere] * 4 + [pl.BlockSpec(memory_space=pltpu.SMEM)],
        out_specs=(vmem, vmem, vmem),
        scratch_shapes=[
            pltpu.VMEM((BLOCK, features), bf16),
            pltpu.VMEM((BLOCK, features), bf16),
            pltpu.VMEM((5, messages, 2, BLOCK, HEAD_DIM), bf16),
            pltpu.VMEM((RETURNED, BLOCK, 5 * BLOCK), f32),
            pltpu.VMEM((RETURNED, BLOCK, 5 * BLOCK), f32),
            pltpu.VMEM((5, 2, 1, BLOCK), f32),
            pltpu.VMEM((5, 2, 1, BLOCK), f32),
            pltpu.VMEM((RETURNED, 3, 1, BLOCK), f32),
            pltpu.VMEM((5, RETURNED, 3, 1, BLOCK), f32),
            pltpu.VMEM((5, RETURNED, 3, 1, BLOCK), f32),
            pltpu.VMEM((RETURNED, 2, 1, BLOCK), f32),
            pltpu.VMEM((5, RETURNED, 2, 1, BLOCK), f32),
            pltpu.VMEM((5, RETURNED, 2, 1, BLOCK), f32),
            pltpu.VMEM((local, 3, 1, BLOCK), f32),
            pltpu.VMEM((5, local, 3, 1, BLOCK), f32),
            pltpu.VMEM((2, RETURNED, HEAD_DIM, BLOCK), f32),
            pltpu.VMEM((5, RETURNED, HEAD_DIM, BLOCK), bf16),
            pltpu.VMEM((5, RETURNED, HEAD_DIM, BLOCK), bf16),
            dma((3, messages)),
            dma((5,)),
            dma((5,)),
            dma((5, messages)),
            dma((5, messages)),
            dma((5, RETURNED)),
            dma((5, RETURNED)),
            dma((5, RETURNED)),
            dma((5, RETURNED)),
            dma((5, local)),
            dma((5, local)),
            dma((5, RETURNED)),
            dma((5, RETURNED)),
        ],
        compiler_params=pltpu.CompilerParams(
            collective_id=0, has_side_effects=True, vmem_limit_bytes=62 << 20
        ),
        cost_estimate=pl.CostEstimate(
            flops=2 * macs,
            bytes_accessed=7 * BLOCK * features * 2,
            transcendentals=heads * 5 * BLOCK * BLOCK,
        ),
    )(queries, key_states, value_states, grad_out, window)

    return pl.pallas_call(
        store,
        out_shape=(out, out, out),
        in_specs=[vmem] * 3,
        out_specs=[anywhere] * 3,
        scratch_shapes=[dma((3,))],
    )(*outs)


def solution(mesh):
    spec = P("tm", "space", None, None)
    return jax.shard_map(
        functools.partial(body, mesh.shape["tm"], mesh.shape["space"]),
        mesh=mesh,
        in_specs=(spec,) * 5,
        out_specs=(spec,) * 3,
        check_vma=False,
    )
```

time: 66.5 us -> 48.6 us (0.73)
  the two profiles are of different devices: /device:TPU:36 before, /device:TPU:121 now
where the time goes in v2:
time: 48.6 us; the launch traced here: 48.4 us
  Pallas kernels  47.8 us (98%)
  between operations  0.64 us (1%)
    pallas_call x1, Pallas kernels, body(): pl.pallas_call(functools.partial(kernel, slabs, bands, heads), out_shape=...  45.5 us
    pallas_call x1, Pallas kernels, body(): pl.pallas_call(store, out_shape=(out, out, out), in_specs=[vmem] * 3, out...  2.26 us

profile of v2, /device:TPU:121, one launch (start us, length us, event | category | flops | bytes accessed | tf_op | source)
XLA Modules:
  0.0 48.4 jit_solution(11119261855695865927)
XLA Ops:
  0.6 45.5 %shard_map.76 = (bf16[1,1,128,1536]{3,2,1,0:T(8,128)(2,1)}, bf16[1,1,128,1536]{3,2,1,0:T(8,128)(2,1)}, bf16[1,1,128,1536]{3,2,1,0:T(8,128)(2,1)}) custom-call(bf16[1,1,128,1536]{3,2,1,0:T(8,128)(2,1)} %q_hbm.1, bf16[1,1,128,1536]{3,2,1,0:T(8,128)(2,1)} %k_hbm.1, bf16[1,1,128,1536]{3,2,1,0:T(8,128)(2,1)} %v_hbm.1, bf16[1,1,128,1536]{3,2,1,0:T(8,128)(2,1)} %g_hbm.1, ...), custom_call_target="tpu_custom_call" | custom-call | flops 1258291200 | bytes 2752512 | tf_op jit(solution)/shard_map/pallas_call | solution.py:511
  46.1 2.3 %shard_map.77 = (bf16[1,1,128,1536]{3,2,1,0:T(8,128)(2,1)}, bf16[1,1,128,1536]{3,2,1,0:T(8,128)(2,1)}, bf16[1,1,128,1536]{3,2,1,0:T(8,128)(2,1)}) custom-call(bf16[1,1,128,1536]{3,2,1,0:T(8,128)(2,1)} %get-tuple-element.6.a, bf16[1,1,128,1536]{3,2,1,0:T(8,128)(2,1)} %get-tuple-element.7.b, bf16[1,1,128,1536]{3,2,1,0:T(8,128)(2,1)} %get-tuple-element.8.c), custom_call_target="tpu_custom_call" | custom-call | tf_op jit(solution)/shard_map/pallas_call | solution.py:559

commit v3 on v2

--- a/solution.py
+++ b/solution.py
@@ -30,10 +30,11 @@
     k_hbm,
     v_hbm,
     g_hbm,
-    window,
+    window_hbm,
     dq_out,
     dk_out,
     dv_out,
+    window,
     k_ref,
     v_ref,
     fw,
@@ -56,7 +57,8 @@
     bias_ssem,
     bias_rsem,
     fwd_ssem,
-    fwd_rsem,
+    x_rsem,
+    arr_rsem,
     st_ssem,
     st_rsem,
     fin_ssem,
@@ -103,34 +105,34 @@
 
     def load(m, h, src, piece):
         return pltpu.make_async_copy(
-            src.at[0, 0, :, head_cols(h)], fw.at[OWN, m, piece], load_sem.at[piece, m]
-        )
-
-    def each_load(m, act):
+            src.at[0, 0, :, head_cols(h)],
+            fw.at[OWN, m, piece],
+            load_sem.at[jnp.where(m < AHEAD, 0, 1)],
+        )
+
+    def start_load(m):
         @pl.when(m < RETURNED)
         def _():
-            act(load(m, m, q_hbm, 0))
-            act(load(m, m, g_hbm, 1))
+            load(m, m, q_hbm, 0).start()
+            load(m, m, g_hbm, 1).start()
 
         @pl.when((m >= RETURNED) & (m < heads))
         def _():
-            act(load(m, m, k_hbm, 0))
-            act(load(m, m, v_hbm, 1))
+            load(m, m, k_hbm, 0).start()
+            load(m, m, v_hbm, 1).start()
 
         @pl.when(m >= heads)
         def _():
-            act(load(m, m - local, q_hbm, 0))
-            act(load(m, m - local, g_hbm, 1))
-
-    k_load = pltpu.make_async_copy(k_hbm.at[0, 0], k_ref, load_sem.at[2, 0])
-    v_load = pltpu.make_async_copy(v_hbm.at[0, 0], v_ref, load_sem.at[2, 1])
-
-    @pl.loop(0, messages)
-    def _(m):
-        each_load(m, lambda copy: copy.start())
-
-    k_load.start()
-    v_load.start()
+            load(m, m - local, q_hbm, 0).start()
+            load(m, m - local, g_hbm, 1).start()
+
+    def wait_load(first, last, sem):
+        span = fw.at[OWN, pl.ds(first, last - first)]
+        pltpu.make_async_copy(span, span, load_sem.at[sem]).wait()
+
+    k_load = pltpu.make_async_copy(k_hbm.at[0, 0], k_ref, load_sem.at[2])
+    v_load = pltpu.make_async_copy(v_hbm.at[0, 0], v_ref, load_sem.at[3])
+    window_load = pltpu.make_async_copy(window_hbm, window, load_sem.at[4])
 
     barrier = pltpu.get_barrier_semaphore()
 
@@ -142,6 +144,94 @@
     guarded(bent, functools.partial(greet, bulk_y))
     guarded(has_zout, functools.partial(greet, zout))
     guarded(has_f, functools.partial(greet, zin))
+
+    @pl.loop(0, AHEAD)
+    def _(m):
+        start_load(m)
+
+    window_load.start()
+
+    count = 2 + 2 * has_f.astype(jnp.int32) + has_y.astype(jnp.int32)
+    count = count + bent.astype(jnp.int32) + has_zout.astype(jnp.int32)
+    pl.semaphore_wait(barrier, count)
+
+    def remote(src, dst, send, recv, device):
+        return pltpu.make_async_remote_copy(
+            src_ref=src,
+            dst_ref=dst,
+            send_sem=send,
+            recv_sem=recv,
+            device_id=device,
+            device_id_type=MESH,
+        )
+
+    def bias_copy(n):
+        return remote(bias_out.at[n], bias_in.at[n], bias_ssem.at[n], bias_rsem.at[0], partner[n])
+
+    def forward(n, m):
+        recv = x_rsem if n == X else arr_rsem
+        return remote(fw.at[OWN, m], fw.at[n, m], fwd_ssem.at[n], recv.at[m], partner[n])
+
+    def bent_forward(m):
+        return remote(fw.at[X, m], fw.at[Y, m], fwd_ssem.at[Y], arr_rsem.at[m], bulk_y)
+
+    def relay(m):
+        return remote(fw.at[X, m], fw.at[F, m], fwd_ssem.at[F], arr_rsem.at[m], zout)
+
+    def st_copy(n, h):
+        return remote(st_out.at[n, h], st_in.at[n, h], st_ssem.at[n], st_rsem.at[h], partner[n])
+
+    def fin_copy(n, h):
+        return remote(
+            fin_out.at[n, h], fin_in.at[n, h], fin_ssem.at[n], fin_rsem.at[h], partner[n]
+        )
+
+    def row_copy(n, j):
+        return remote(row_own.at[j], row_in.at[n, j], row_ssem.at[n], row_rsem.at[j], partner[n])
+
+    def dq_copy(n, h):
+        device = {C: partner[C], Y: bulk_y, X: partner[X], F: zin}[n]
+        whose = {C: 0, Y: jnp.where(bent, 1, 0), X: 0, F: 1}[n]
+        return remote(
+            dq_send.at[n, h], dq_in.at[n, h], dq_ssem.at[n], dq_rsem.at[whose, h], device
+        )
+
+    def landed(span, sem):
+        remote(span, span, fwd_ssem.at[OWN], sem, partner[C]).wait_recv()
+
+    def sent(span, sem):
+        remote(span, span, sem, x_rsem.at[0], partner[C]).wait_send()
+
+    def by_count(least, act):
+        for more, condition in (
+            (2, has_y & has_f),
+            (1, has_y != has_f),
+            (0, jnp.logical_not(has_y | has_f)),
+        ):
+            pl.when(condition)(functools.partial(act, least + more))
+
+    def send_own(m):
+        forward(X, m).start()
+        forward(C, m).start()
+
+        @pl.when(straight)
+        def _():
+            forward(Y, m).start()
+
+    wait_load(0, AHEAD, 0)
+
+    @pl.loop(0, AHEAD)
+    def _(m):
+        send_own(m)
+
+    @pl.loop(AHEAD, messages)
+    def _(m):
+        start_load(m)
+
+    k_load.start()
+    v_load.start()
+
+    window_load.wait()
 
     lane_tile = lax.broadcasted_iota(jnp.int32, (1, BLOCK), 1) // TILE_TOKENS
     dirs = {
@@ -173,6 +263,9 @@
             else:
                 bias_out[n, key_tile] = row
 
+    for n in (X, F, C, Y):
+        guarded(present[n], lambda n=n: bias_copy(n).start())
+
     def blank(n):
         bias_in[n] = jnp.zeros_like(bias_in[n])
 
@@ -206,78 +299,6 @@
         def _(h):
             dq_in[F, h] = jnp.zeros(dq_in.shape[2:], dq_in.dtype)
 
-    count = 2 + 2 * has_f.astype(jnp.int32) + has_y.astype(jnp.int32)
-    count = count + bent.astype(jnp.int32) + has_zout.astype(jnp.int32)
-    pl.semaphore_wait(barrier, count)
-
-    def remote(src, dst, send, recv, device):
-        return pltpu.make_async_remote_copy(
-            src_ref=src,
-            dst_ref=dst,
-            send_sem=send,
-            recv_sem=recv,
-            device_id=device,
-            device_id_type=MESH,
-        )
-
-    def bias_copy(n):
-        return remote(
-            bias_out.at[n], bias_in.at[n], bias_ssem.at[n], bias_rsem.at[n], partner[n]
-        )
-
-    def forward(n, c):
-        return remote(
-            fw.at[OWN, c], fw.at[n, c], fwd_ssem.at[n, c], fwd_rsem.at[n, c], partner[n]
-        )
-
-    def bent_forward(c):
-        return remote(fw.at[X, c], fw.at[Y, c], fwd_ssem.at[Y, c], fwd_rsem.at[Y, c], bulk_y)
-
-    def relay(c):
-        return remote(fw.at[X, c], fw.at[F, c], fwd_ssem.at[F, c], fwd_rsem.at[F, c], zout)
-
-    def st_copy(n, c):
-        return remote(
-            st_out.at[n, c], st_in.at[n, c], st_ssem.at[n, c], st_rsem.at[n, c], partner[n]
-        )
-
-    def fin_copy(n, c):
-        return remote(
-            fin_out.at[n, c], fin_in.at[n, c], fin_ssem.at[n, c], fin_rsem.at[n, c], partner[n]
-        )
-
-    def row_copy(n, j):
-        return remote(
-            row_own.at[j], row_in.at[n, j], row_ssem.at[n, j], row_rsem.at[n, j], partner[n]
-        )
-
-    def dq_copy(n, c):
-        device = {C: partner[C], Y: bulk_y, X: partner[X], F: zin}[n]
-        return remote(
-            dq_send.at[n, c], dq_in.at[n, c], dq_ssem.at[n, c], dq_rsem.at[n, c], device
-        )
-
-    for n in (X, F, C, Y):
-        guarded(present[n], lambda n=n: bias_copy(n).start())
-
-    def send_own(m):
-        each_load(m, lambda copy: copy.wait())
-        forward(X, m).start()
-        forward(C, m).start()
-
-        @pl.when(straight)
-        def _():
-            forward(Y, m).start()
-
-    @pl.loop(0, AHEAD)
-    def _(m):
-        send_own(m)
-
-    k_load.wait()
-    v_load.wait()
-    for n in (X, F, C, Y):
-        guarded(present[n], lambda n=n: bias_copy(n).wait_recv())
-
     def nearby(m, piece):
         return jnp.concatenate([fw[n, m, piece] for n in range(5)], axis=0)
 
@@ -296,23 +317,14 @@
         )
 
     def arrived(m):
-        forward(C, m).wait_recv()
-
-        @pl.when(has_y)
-        def _():
-            forward(Y, m).wait_recv()
-
-        @pl.when(has_f)
-        def _():
-            relay(m).wait_recv()
+        by_count(1, lambda count: landed(fw.at[pl.ds(1, count), m], arr_rsem.at[m]))
 
     def to_neighbours(copy, at):
         for n in (F, X, Y, C):
             guarded(present[n], lambda n=n: copy(n, at).start())
 
-    def from_neighbours(copy, at):
-        for n in (C, Y, X, F):
-            guarded(present[n], lambda n=n: copy(n, at).wait_recv())
+    def from_neighbours(buffer, at, sem):
+        by_count(2, lambda count: landed(buffer.at[pl.ds(1, count), at], sem.at[at]))
 
     def stage_relay(m):
         forward(X, m).wait_recv()
@@ -350,7 +362,7 @@
         to_neighbours(st_copy, h)
 
     def stage_combine(h):
-        from_neighbours(st_copy, h)
+        from_neighbours(st_in, h, st_rsem)
         tops, totals, mixes = (
             [st_own[h, at]] + [st_in[n, h, at] for n in (C, Y, X, F)] for at in range(3)
         )
@@ -374,7 +386,7 @@
         return grad_scores
 
     def stage_phase2(h):
-        from_neighbours(fin_copy, h)
+        from_neighbours(fin_in, h, fin_rsem)
         cols = head_cols(h)
         factor, delta = (
             jnp.concatenate([fin_own[h, at]] + [fin_in[n, h, at] for n in (C, Y, X, F)], axis=1)
@@ -391,11 +403,16 @@
         dq_copy(C, h).start()
 
     def stage_xret(h):
-        guarded(has_zout, lambda: dq_copy(F, h).wait_recv())
+        @pl.when(has_zout & bent)
+        def _():
+            landed(dq_in.at[pl.ds(1, 2), h], dq_rsem.at[1, h])
+
+        @pl.when(has_zout != bent)
+        def _():
+            landed(dq_in.at[pl.ds(1, 1), h], dq_rsem.at[1, h])
 
         @pl.when(bent)
         def _():
-            dq_copy(Y, h).wait_recv()
             dq_own[1, h] = dq_own[1, h] + dq_in[Y, h].astype(jnp.float32)
             dq_in[Y, h] = jnp.zeros(dq_in.shape[2:], dq_in.dtype)
 
@@ -403,9 +420,14 @@
         dq_copy(X, h).start()
 
     def stage_final(h):
-        dq_copy(C, h).wait_recv()
-        guarded(straight, lambda: dq_copy(Y, h).wait_recv())
-        dq_copy(X, h).wait_recv()
+        @pl.when(straight)
+        def _():
+            landed(dq_in.at[pl.ds(1, 3), h], dq_rsem.at[0, h])
+
+        @pl.when(jnp.logical_not(straight))
+        def _():
+            landed(dq_in.at[pl.ds(1, 2), h], dq_rsem.at[0, h])
+
         total = dq_own[0, h]
         for n in (C, Y, X):
             total = total + dq_in[n, h].astype(jnp.float32)
@@ -440,7 +462,7 @@
     def stage_own_keys(j):
         kv, qg = RETURNED + j, heads + j
         arrived(qg)
-        from_neighbours(row_copy, j)
+        from_neighbours(row_in, j, row_rsem)
         top, inverse, delta = (
             jnp.concatenate([row_own[j, at]] + [row_in[n, j, at] for n in (C, Y, X, F)], axis=1)
             for at in range(3)
@@ -461,31 +483,34 @@
         (LAG_ARRIVED + heads, local, stage_own_keys),
     )
 
+    wait_load(AHEAD, messages, 1)
+
     @pl.loop(0, max(messages + LAG_ARRIVED, RETURNED + LAG_FINAL))
     def _(tick):
+        @pl.when(tick == LAG_ARRIVED)
+        def _():
+            k_load.wait()
+            v_load.wait()
+            by_count(2, lambda count: landed(bias_in.at[pl.ds(1, count)], bias_rsem.at[0]))
+
         for lag, count, stage in stages:
 
             @pl.when((tick >= lag) & (tick < count + lag))
             def _(lag=lag, stage=stage):
                 stage(tick - lag)
 
-    for n in (X, F, C, Y):
-        guarded(present[n], lambda n=n: bias_copy(n).wait_send())
-
-    @pl.loop(0, messages)
-    def _(m):
-        forward(X, m).wait_send()
-        forward(C, m).wait_send()
-        guarded(has_y, lambda: bent_forward(m).wait_send())
-        guarded(has_zout, lambda: relay(m).wait_send())
-
-    for count, copies in ((RETURNED, (st_copy, fin_copy, dq_copy)), (local, (row_copy,))):
-
-        @pl.loop(0, count)
-        def _(at, copies=copies):
-            for copy in copies:
-                for n in (C, Y, X, F):
-                    guarded(present[n], lambda n=n, copy=copy: copy(n, at).wait_send())
+    for n, condition in ((X, None), (C, None), (Y, has_y), (F, has_zout)):
+        guarded(condition, lambda n=n: sent(fw.at[OWN], fwd_ssem.at[n]))
+
+    def wait_sends(n):
+        sent(bias_out.at[n], bias_ssem.at[n])
+        sent(st_out.at[n], st_ssem.at[n])
+        sent(fin_out.at[n], fin_ssem.at[n])
+        sent(row_own, row_ssem.at[n])
+        sent(dq_send.at[n], dq_ssem.at[n])
+
+    for n in (C, Y, X, F):
+        guarded(present[n], functools.partial(wait_sends, n))
 
 
 def store(a, b, c, a_out, b_out, c_out, sems):
@@ -510,10 +535,11 @@
     macs = heads * 5 * 5 * BLOCK * BLOCK * HEAD_DIM
     outs = pl.pallas_call(
         functools.partial(kernel, slabs, bands, heads),
-        out_shape=(out, out, out),
-        in_specs=[anywhere] * 4 + [pl.BlockSpec(memory_space=pltpu.SMEM)],
+        out_shape=(pltpu.VMEM(queries.shape, bf16),) * 3,
+        in_specs=[anywhere] * 5,
         out_specs=(vmem, vmem, vmem),
         scratch_shapes=[
+            pltpu.SMEM(window.shape, jnp.int32),
             pltpu.VMEM((BLOCK, features), bf16),
             pltpu.VMEM((BLOCK, features), bf16),
             pltpu.VMEM((5, messages, 2, BLOCK, HEAD_DIM), bf16),
@@ -532,22 +558,23 @@
             pltpu.VMEM((2, RETURNED, HEAD_DIM, BLOCK), f32),
             pltpu.VMEM((5, RETURNED, HEAD_DIM, BLOCK), bf16),
             pltpu.VMEM((5, RETURNED, HEAD_DIM, BLOCK), bf16),
-            dma((3, messages)),
             dma((5,)),
             dma((5,)),
-            dma((5, messages)),
-            dma((5, messages)),
-            dma((5, RETURNED)),
-            dma((5, RETURNED)),
-            dma((5, RETURNED)),
-            dma((5, RETURNED)),
-            dma((5, local)),
-            dma((5, local)),
-            dma((5, RETURNED)),
-            dma((5, RETURNED)),
+            dma((1,)),
+            dma((5,)),
+            dma((messages,)),
+            dma((messages,)),
+            dma((5,)),
+            dma((RETURNED,)),
+            dma((5,)),
+            dma((RETURNED,)),
+            dma((5,)),
+            dma((local,)),
+            dma((5,)),
+            dma((2, RETURNED)),
         ],
         compiler_params=pltpu.CompilerParams(
-            collective_id=0, has_side_effects=True, vmem_limit_bytes=62 << 20
+            collective_id=0, has_side_effects=True, vmem_limit_bytes=58 << 20
         ),
         cost_estimate=pl.CostEstimate(
             flops=2 * macs,
@@ -562,6 +589,7 @@
         in_specs=[vmem] * 3,
         out_specs=[anywhere] * 3,
         scratch_shapes=[dma((3,))],
+        compiler_params=pltpu.CompilerParams(vmem_limit_bytes=8 << 20),
     )(*outs)
 
 

time: 48.6 us -> 41.9 us (0.86)
  Pallas kernels: 47.8 us -> 41.1 us
    pallas_call x1, Pallas kernels: 45.5 us -> 40.1 us  [body(): pl.pallas_call(functools.partial(kernel, slabs, bands, heads), out_shape=...]
    pallas_call x1, Pallas kernels: 2.26 us -> 1.03 us  [body(): pl.pallas_call(store, out_shape=(out, out, out), in_specs=[vmem] * 3, out...]
where the time goes in v3:
time: 41.9 us; the launch traced here: 41.7 us
  Pallas kernels  41.1 us (98%)
  between operations  0.64 us (2%)
    pallas_call x1, Pallas kernels, body(): pl.pallas_call(functools.partial(kernel, slabs, bands, heads), out_shape=...  40.1 us
    pallas_call x1, Pallas kernels, body(): pl.pallas_call(store, out_shape=(out, out, out), in_specs=[vmem] * 3, out...  1.03 us

profile of v3, /device:TPU:121, one launch (start us, length us, event | category | flops | bytes accessed | tf_op | source)
XLA Modules:
  0.0 41.7 jit_solution(17734164574390357828)
XLA Ops:
  0.6 40.1 %shard_map.76 = (bf16[1,1,128,1536]{3,2,1,0:T(8,128)(2,1)S(1)}, bf16[1,1,128,1536]{3,2,1,0:T(8,128)(2,1)S(1)}, bf16[1,1,128,1536]{3,2,1,0:T(8,128)(2,1)S(1)}) custom-call(bf16[1,1,128,1536]{3,2,1,0:T(8,128)(2,1)} %q_hbm.1, bf16[1,1,128,1536]{3,2,1,0:T(8,128)(2,1)} %k_hbm.1, bf16[1,1,128,1536]{3,2,1,0:T(8,128)(2,1)} %v_hbm.1, ...), custom_call_target="tpu_custom_call" | custom-call | flops 1258291200 | bytes 2752512 | tf_op jit(solution)/shard_map/pallas_call | solution.py:536
  40.7 1.0 %shard_map.77 = (bf16[1,1,128,1536]{3,2,1,0:T(8,128)(2,1)}, bf16[1,1,128,1536]{3,2,1,0:T(8,128)(2,1)}, bf16[1,1,128,1536]{3,2,1,0:T(8,128)(2,1)}) custom-call(bf16[1,1,128,1536]{3,2,1,0:T(8,128)(2,1)S(1)} %get-tuple-element.6.a, bf16[1,1,128,1536]{3,2,1,0:T(8,128)(2,1)S(1)} %get-tuple-element.7.b, bf16[1,1,128,1536]{3,2,1,0:T(8,128)(2,1)S(1)} %get-tuple-element.8.c), custom_call_target="tpu_custom_call" | custom-call | tf_op jit(solution)/shard_map/pallas_call | solution.py:586

commit v4 on v0

v4 whole, which is shorter than its diff:
```python
import functools
import math

import jax
import jax.numpy as jnp
from jax import lax
from jax.experimental import pallas as pl
from jax.experimental.pallas import tpu as pltpu
from jax.sharding import PartitionSpec as P

MESH = pl.DeviceIdType.MESH
HEAD_DIM = 128
TILE_TOKENS = 64
BLOCK = 128
MASKED = -1e30
SCALE = HEAD_DIM ** (-0.5)
SCALE_LOG2E = SCALE * math.log2(math.e)

OWN, C, Y, X, F = range(5)
G, H = 1, 2
PAIRS = (OWN, C, X, Y, F)
AHEAD = 3
LAG_SCORES, LAG_COMBINE, LAG_GRADS, LAG_RETURN, LAG_FINAL = 1, 3, 5, 8, 12


def kernel(
    slabs,
    bands,
    heads,
    q_hbm,
    k_hbm,
    v_hbm,
    g_hbm,
    window_hbm,
    dq_out,
    dk_out,
    dv_out,
    window,
    fw,
    kv,
    weight,
    gprob,
    tops,
    bias_out,
    bias_in,
    bias_x,
    st_own,
    st_out,
    st_in,
    fin_own,
    fin_in,
    dq_own,
    dq_send,
    dq_in,
    dkv_own,
    dkv_send,
    dkv_in,
    load_sem,
    bias_ssem,
    bias_rsem,
    fwd_ssem,
    x_rsem,
    arr_rsem,
    st_ssem,
    st_rsem,
    fin_ssem,
    fin_rsem,
    dq_ssem,
    dq_rsem,
    dkv_ssem,
    dkv_rsem,
):
    t = lax.axis_index("tm")
    b = lax.axis_index("space")
    tstep = 2 * lax.rem(t, 2) - 1
    bstep = 1 - 2 * lax.rem(b, 2)
    t_c, t_y = t - tstep, t + tstep
    b_x, b_f = b + bstep, b - bstep
    b_zout, b_zin = b + 2 * bstep, b - 2 * bstep
    has_y = (t_y >= 0) & (t_y < slabs)
    has_f = (b_f >= 0) & (b_f < bands)
    has_zout = (b_zout >= 0) & (b_zout < bands)
    bent = (t == slabs // 2 - 1) | (t == slabs // 2)
    straight = has_y & jnp.logical_not(bent)

    partner = {C: (t_c, b), Y: (t_y, b), X: (t, b_x)}
    reached = {C: None, Y: straight, X: None}
    across, zout, zin = (t_y, b_x), (t, b_zout), (t, b_zin)

    def guarded(condition, action):
        if condition is None:
            action()
        else:
            pl.when(condition)(action)

    def cols(h):
        return pl.ds(pl.multiple_of(h * HEAD_DIM, HEAD_DIM), HEAD_DIM)

    def start_load(h):
        sem = load_sem.at[jnp.where(h < AHEAD, 0, 1)]
        for src, dst in (
            (q_hbm, fw.at[OWN, h, 0]),
            (g_hbm, fw.at[OWN, h, 1]),
            (k_hbm, kv.at[OWN, h, 0]),
            (v_hbm, kv.at[OWN, h, 1]),
        ):
            pltpu.make_async_copy(src.at[0, 0, :, cols(h)], dst, sem).start()

    def wait_load(first, last, sem):
        span = pl.ds(first, last - first)
        both = fw.at[pl.ds(0, 2), span]
        pltpu.make_async_copy(both, both, load_sem.at[sem]).wait()

    window_load = pltpu.make_async_copy(window_hbm, window, load_sem.at[2])

    barrier = pltpu.get_barrier_semaphore()

    def greet(device):
        pl.semaphore_signal(barrier, inc=1, device_id=device, device_id_type=MESH)

    for device, condition in (
        (partner[X], None),
        (partner[C], None),
        (partner[Y], straight),
        (across, bent),
        (zout, has_zout),
        (zin, has_f),
    ):
        guarded(condition, functools.partial(greet, device))

    @pl.loop(0, AHEAD)
    def _(h):
        start_load(h)

    window_load.start()
    count = 2 + has_y.astype(jnp.int32) + has_f.astype(jnp.int32) + has_zout.astype(jnp.int32)
    pl.semaphore_wait(barrier, count)

    def remote(src, dst, send, recv, device):
        return pltpu.make_async_remote_copy(
            src_ref=src,
            dst_ref=dst,
            send_sem=send,
            recv_sem=recv,
            device_id=device,
            device_id_type=MESH,
        )

    def bias_copy(n):
        if n == X:
            return remote(bias_out, bias_x, bias_ssem.at[X], bias_rsem.at[1], partner[X])
        return remote(bias_out.at[n], bias_in.at[n], bias_ssem.at[n], bias_rsem.at[0], partner[n])

    def send_x(h, piece):
        remote(
            fw.at[OWN, h, piece],
            fw.at[X, h, piece],
            fwd_ssem.at[X],
            x_rsem.at[h],
            partner[X],
        ).start()

    def send_own(h):
        send_x(h, 0)
        recv = arr_rsem.at[h]

        @pl.when(has_f)
        def _():
            remote(kv.at[OWN, h], kv.at[G, h], fwd_ssem.at[F], recv, zin).start()

        @pl.when(bent)
        def _():
            remote(kv.at[OWN, h], kv.at[H, h], fwd_ssem.at[Y], recv, across).start()

        @pl.when(straight)
        def _():
            remote(fw.at[OWN, h], fw.at[Y, h], fwd_ssem.at[Y], recv, partner[Y]).start()

        remote(fw.at[OWN, h], fw.at[C, h], fwd_ssem.at[C], recv, partner[C]).start()

    def send_st(n, h):
        remote(
            st_out.at[n, h], st_in.at[n, h], st_ssem.at[n], st_rsem.at[h], partner[n]
        ).start()

    def send_fin(n, h):
        remote(fin_own.at[h], fin_in.at[n, h], fin_ssem.at[n], fin_rsem.at[h], partner[n]).start()

    def send_dq(n, h):
        remote(
            dq_send.at[n, h], dq_in.at[n, h], dq_ssem.at[n], dq_rsem.at[h], partner[n]
        ).start()

    def send_dkv(at, h, device):
        remote(
            dkv_send.at[at, h], dkv_in.at[at, h], dkv_ssem.at[at], dkv_rsem.at[h], device
        ).start()

    def landed(span, sem):
        remote(span, span, fwd_ssem.at[OWN], sem, partner[C]).wait_recv()

    def sent(span, sem):
        remote(span, span, sem, x_rsem.at[0], partner[C]).wait_send()

    def by_count(least, first, second, act):
        for more, condition in (
            (2, first & second),
            (1, first != second),
            (0, jnp.logical_not(first | second)),
        ):
            if least + more:
                pl.when(condition)(functools.partial(act, least + more))

    def from_reached(buffer, h, sem):
        @pl.when(straight)
        def _():
            landed(buffer.at[pl.ds(1, 3), h], sem.at[h])

        @pl.when(jnp.logical_not(straight))
        def _():
            landed(buffer.at[pl.ds(1, 2), h], sem.at[h])

    def to_reached(send, h):
        for n in (X, Y, C):
            guarded(reached[n], functools.partial(send, n, h))

    wait_load(0, AHEAD, 0)

    @pl.loop(0, AHEAD)
    def _(h):
        send_own(h)
        send_x(h, 1)

    @pl.loop(AHEAD, heads)
    def _(h):
        start_load(h)

    window_load.wait()

    lane_tile = lax.broadcasted_iota(jnp.int32, (1, BLOCK), 1) // TILE_TOKENS
    present = {Y: has_y, F: has_f}
    dirs = {
        OWN: (0, 0),
        C: (-tstep, 0),
        Y: (tstep, 0),
        X: (0, bstep),
        F: (0, -bstep),
    }
    for n in (OWN, C, Y, X, F):
        dt, dr = dirs[n]
        for key_tile in range(2):
            row = None
            for query_tile in range(2):
                dc = key_tile - query_tile
                if n == OWN and dc == 0:
                    value = jnp.float32(0.0)
                else:
                    code = 9 * (dt + 1) + 3 * (dr + 1) + dc + 1
                    listed = window[0, 0, query_tile, code]
                    shown = listed == 1
                    if n in present:
                        shown = shown & present[n]
                    value = jnp.where(shown, 0.0, MASKED).astype(jnp.float32)
                part = jnp.full((1, BLOCK), value, jnp.float32)
                row = part if row is None else jnp.where(lane_tile == 0, row, part)
            bias_out[n, key_tile] = row

    for n in (X, C, Y):
        guarded(reached[n], lambda n=n: bias_copy(n).start())

    zero_row = jnp.zeros((1, BLOCK), jnp.float32)

    @pl.when(jnp.logical_not(straight))
    def _():
        bias_in[Y] = jnp.zeros_like(bias_in[Y])

        @pl.loop(0, heads)
        def _(h):
            fw[Y, h] = jnp.zeros(fw.shape[2:], fw.dtype)
            st_in[Y, h, 0] = jnp.full((1, BLOCK), MASKED, jnp.float32)
            for at in (1, 2):
                st_in[Y, h, at] = zero_row
            for at in range(3):
                fin_in[Y, h, at] = zero_row
            dq_in[Y, h] = jnp.zeros(dq_in.shape[2:], dq_in.dtype)

    @pl.when(jnp.logical_not(has_zout))
    def _():
        @pl.loop(0, heads)
        def _(h):
            kv[G, h] = jnp.zeros(kv.shape[2:], kv.dtype)

    for at, condition in ((0, has_f), (1, bent)):

        @pl.when(jnp.logical_not(condition))
        def _(at=at):
            @pl.loop(0, heads)
            def _(h):
                dkv_in[at, h] = jnp.zeros(dkv_in.shape[2:], dkv_in.dtype)

    y_queries = jnp.where(bent, X, Y)
    y_keys = jnp.where(bent, H, OWN)

    def dot(a, b, a_dim, b_dim):
        return lax.dot_general(
            a, b, (((a_dim,), (b_dim,)), ((), ())), preferred_element_type=jnp.float32
        )

    def thrice(h, piece):
        return jnp.concatenate([fw[n, h, piece] for n in (OWN, C, X)], axis=0)

    def products(h, piece):
        return jnp.concatenate(
            [
                dot(kv[OWN, h, piece], thrice(h, piece), 1, 1),
                dot(kv[y_keys, h, piece], fw[y_queries, h, piece], 1, 1),
                dot(kv[G, h, piece], fw[X, h, piece], 1, 1),
            ],
            axis=1,
        )

    def split(row):
        return {n: row[:, i * BLOCK : (i + 1) * BLOCK] for i, n in enumerate(PAIRS)}

    def merged(parts):
        top = functools.reduce(jnp.maximum, [part[0] for part in parts])
        shares = [jnp.exp2((part[0] - top) * SCALE_LOG2E) for part in parts]
        total, mixed = (
            sum(share * part[at] for share, part in zip(shares, parts)) for at in (1, 2)
        )
        return top, total, mixed

    def stage_scores(h):
        by_count(1, has_y, has_zout, lambda count: landed(fw.at[pl.ds(0, count), h], arr_rsem.at[h]))
        masks = []
        for key_tile in range(2):
            y_mask = jnp.where(bent, bias_x[Y, key_tile], bias_in[Y, key_tile])
            rows = [bias_out[OWN, key_tile], bias_in[C, key_tile], bias_x[X, key_tile]]
            masks.append(jnp.concatenate(rows + [y_mask, bias_x[F, key_tile]], axis=1))
        scores = products(h, 0)
        scores = jnp.concatenate(
            [scores[:TILE_TOKENS] + masks[0], scores[TILE_TOKENS:] + masks[1]], axis=0
        )
        top = jnp.max(scores, axis=0, keepdims=True)
        powers = jnp.exp2((scores - top) * SCALE_LOG2E)
        weight[h] = powers
        total = jnp.sum(powers, axis=0, keepdims=True)
        grad_probs = products(h, 1)
        gprob[h] = grad_probs
        mixed = jnp.sum(powers * grad_probs, axis=0, keepdims=True)
        top, total, mixed = split(top), split(total), split(mixed)
        for i, n in enumerate(PAIRS):
            tops[h, i] = top[n]
        part = {n: (top[n], total[n], mixed[n]) for n in PAIRS}
        y_part = (jnp.where(bent, top[Y], MASKED),) + tuple(
            jnp.where(bent, row[Y], 0.0) for row in (total, mixed)
        )
        x_part = merged([part[X], part[F], y_part])
        for at in range(3):
            st_own[h, at] = part[OWN][at]
            st_out[C, h, at] = part[C][at]
            st_out[Y, h, at] = part[Y][at]
            st_out[X, h, at] = x_part[at]
        to_reached(send_st, h)

    def stage_combine(h):
        from_reached(st_in, h, st_rsem)
        parts = [tuple(st_own[h, at] for at in range(3))]
        parts += [tuple(st_in[n, h, at] for at in range(3)) for n in (C, Y, X)]
        top, total, mixed = merged(parts)
        inverse = 1.0 / total
        for at, row in enumerate((top, inverse, mixed * inverse)):
            fin_own[h, at] = row
        to_reached(send_fin, h)

    def stage_grads(h):
        from_reached(fin_in, h, fin_rsem)
        top, inverse, delta = (
            jnp.concatenate(
                [
                    fin_own[h, at],
                    fin_in[C, h, at],
                    fin_in[X, h, at],
                    jnp.where(bent, fin_in[X, h, at], fin_in[Y, h, at]),
                    fin_in[X, h, at],
                ],
                axis=1,
            )
            for at in range(3)
        )
        own_top = jnp.concatenate([tops[h, i] for i in range(5)], axis=1)
        factor = jnp.exp2((own_top - top) * SCALE_LOG2E) * inverse
        probs = weight[h] * factor
        grad_scores = (probs * ((gprob[h] - delta) * SCALE)).astype(jnp.bfloat16)
        probs = probs.astype(jnp.bfloat16)
        third, fourth = 3 * BLOCK, 4 * BLOCK
        own_scores = grad_scores[:, :third]
        y_scores = grad_scores[:, third:fourth]
        g_scores = grad_scores[:, fourth:]
        turned = dot(kv[OWN, h, 0], own_scores, 0, 0)
        y_turned = dot(kv[y_keys, h, 0], y_scores, 0, 0)
        g_turned = dot(kv[G, h, 0], g_scores, 0, 0)
        dq_own[h] = turned[:, :BLOCK]
        dq_send[C, h] = turned[:, BLOCK : 2 * BLOCK].astype(jnp.bfloat16)
        dq_send[Y, h] = y_turned.astype(jnp.bfloat16)
        x_turned = turned[:, 2 * BLOCK :] + g_turned + jnp.where(bent, y_turned, 0.0)
        dq_send[X, h] = x_turned.astype(jnp.bfloat16)
        guarded(straight, lambda: send_dq(Y, h))
        send_dq(C, h)
        for piece, left in enumerate((grad_scores, probs)):
            own = dot(left[:, :third], thrice(h, piece), 1, 0)
            from_y = dot(left[:, third:fourth], fw[y_queries, h, piece], 1, 0)
            from_g = dot(left[:, fourth:], fw[X, h, piece], 1, 0)
            dkv_own[h, piece] = own + jnp.where(bent, 0.0, from_y)
            dkv_send[0, h, piece] = from_g.astype(jnp.bfloat16)
            dkv_send[1, h, piece] = from_y.astype(jnp.bfloat16)
        guarded(has_zout, lambda: send_dkv(0, h, zout))
        guarded(bent, lambda: send_dkv(1, h, across))

    def stage_return(h):
        send_dq(X, h)

    def stage_final(h):
        from_reached(dq_in, h, dq_rsem)
        total = dq_own[h]
        for n in (C, Y, X):
            total = total + dq_in[n, h].astype(jnp.float32)
        dq_out[0, 0, :, cols(h)] = total.T.astype(jnp.bfloat16)
        by_count(0, has_f, bent, lambda count: landed(dkv_in.at[pl.ds(0, count), h], dkv_rsem.at[h]))
        for piece, out in enumerate((dk_out, dv_out)):
            total = dkv_own[h, piece]
            for at in range(2):
                total = total + dkv_in[at, h, piece].astype(jnp.float32)
            out[0, 0, :, cols(h)] = total.astype(jnp.bfloat16)

    def stage_arrival(h):
        landed(fw.at[X, h], x_rsem.at[h])

        @pl.when(h + AHEAD < heads)
        def _():
            send_own(h + AHEAD)

    def stage_second_piece(h):
        @pl.when(h + AHEAD < heads)
        def _():
            send_x(h + AHEAD, 1)

    wait_load(AHEAD, heads, 1)
    stages = (
        (0, stage_arrival),
        (LAG_SCORES, stage_scores),
        (LAG_COMBINE, stage_combine),
        (0, stage_second_piece),
        (LAG_FINAL, stage_final),
        (LAG_RETURN, stage_return),
        (LAG_GRADS, stage_grads),
    )

    @pl.loop(0, heads + LAG_FINAL)
    def _(tick):
        @pl.when(tick == LAG_SCORES)
        def _():
            landed(bias_x, bias_rsem.at[1])

            @pl.when(straight)
            def _():
                landed(bias_in.at[pl.ds(1, 2)], bias_rsem.at[0])

            @pl.when(jnp.logical_not(straight))
            def _():
                landed(bias_in.at[pl.ds(1, 1)], bias_rsem.at[0])

        for lag, stage in stages:

            @pl.when((tick >= lag) & (tick < heads + lag))
            def _(lag=lag, stage=stage):
                stage(tick - lag)

    for n, condition in ((X, None), (C, None), (Y, has_y), (F, has_f)):
        guarded(condition, lambda n=n: sent(fw.at[OWN], fwd_ssem.at[n]))

    def wait_sends(n):
        sent(bias_out if n == X else bias_out.at[n], bias_ssem.at[n])
        sent(st_out.at[n], st_ssem.at[n])
        sent(fin_own, fin_ssem.at[n])
        sent(dq_send.at[n], dq_ssem.at[n])

    for n in (C, Y, X):
        guarded(reached[n], functools.partial(wait_sends, n))
    guarded(has_zout, lambda: sent(dkv_send.at[0], dkv_ssem.at[0]))
    guarded(bent, lambda: sent(dkv_send.at[1], dkv_ssem.at[1]))


def store(a, b, c, a_out, b_out, c_out, sems):
    pairs = ((a, a_out), (b, b_out), (c, c_out))
    copies = [pltpu.make_async_copy(x, y, sems.at[i]) for i, (x, y) in enumerate(pairs)]
    for copy in copies:
        copy.start()
    for copy in copies:
        copy.wait()


def body(slabs, bands, queries, key_states, value_states, grad_out, window):
    features = queries.shape[3]
    heads = features // HEAD_DIM
    f32, bf16 = jnp.float32, jnp.bfloat16
    dma = pltpu.SemaphoreType.DMA
    out = jax.ShapeDtypeStruct(queries.shape, bf16)
    anywhere = pl.BlockSpec(memory_space=pl.ANY)
    vmem = pl.BlockSpec(memory_space=pltpu.VMEM)
    macs = heads * 5 * 5 * BLOCK * BLOCK * HEAD_DIM
    outs = pl.pallas_call(
        functools.partial(kernel, slabs, bands, heads),
        out_shape=(pltpu.VMEM(queries.shape, bf16),) * 3,
        in_specs=[anywhere] * 5,
        out_specs=(vmem, vmem, vmem),
        scratch_shapes=[
            pltpu.SMEM(window.shape, jnp.int32),
            pltpu.VMEM((4, heads, 2, BLOCK, HEAD_DIM), bf16),
            pltpu.VMEM((3, heads, 2, BLOCK, HEAD_DIM), bf16),
            pltpu.VMEM((heads, BLOCK, 5 * BLOCK), f32),
            pltpu.VMEM((heads, BLOCK, 5 * BLOCK), f32),
            pltpu.VMEM((heads, 5, 1, BLOCK), f32),
            pltpu.VMEM((5, 2, 1, BLOCK), f32),
            pltpu.VMEM((3, 2, 1, BLOCK), f32),
            pltpu.VMEM((5, 2, 1, BLOCK), f32),
            pltpu.VMEM((heads, 3, 1, BLOCK), f32),
            pltpu.VMEM((4, heads, 3, 1, BLOCK), f32),
            pltpu.VMEM((4, heads, 3, 1, BLOCK), f32),
            pltpu.VMEM((heads, 3, 1, BLOCK), f32),
            pltpu.VMEM((4, heads, 3, 1, BLOCK), f32),
            pltpu.VMEM((heads, HEAD_DIM, BLOCK), f32),
            pltpu.VMEM((4, heads, HEAD_DIM, BLOCK), bf16),
            pltpu.VMEM((4, heads, HEAD_DIM, BLOCK), bf16),
            pltpu.VMEM((heads, 2, BLOCK, HEAD_DIM), f32),
            pltpu.VMEM((2, heads, 2, BLOCK, HEAD_DIM), bf16),
            pltpu.VMEM((2, heads, 2, BLOCK, HEAD_DIM), bf16),
            dma((3,)),
            dma((4,)),
            dma((2,)),
            dma((5,)),
            dma((heads,)),
            dma((heads,)),
            dma((4,)),
            dma((heads,)),
            dma((4,)),
            dma((heads,)),
            dma((4,)),
            dma((heads,)),
            dma((2,)),
            dma((heads,)),
        ],
        compiler_params=pltpu.CompilerParams(
            collective_id=0, has_side_effects=True, vmem_limit_bytes=58 << 20
        ),
        cost_estimate=pl.CostEstimate(
            flops=2 * macs,
            bytes_accessed=7 * BLOCK * features * 2,
            transcendentals=heads * 5 * BLOCK * BLOCK,
        ),
    )(queries, key_states, value_states, grad_out, window)

    return pl.pallas_call(
        store,
        out_shape=(out, out, out),
        in_specs=[vmem] * 3,
        out_specs=[anywhere] * 3,
        scratch_shapes=[dma((3,))],
        compiler_params=pltpu.CompilerParams(vmem_limit_bytes=8 << 20),
    )(*outs)


def solution(mesh):
    spec = P("tm", "space", None, None)
    return jax.shard_map(
        functools.partial(body, mesh.shape["tm"], mesh.shape["space"]),
        mesh=mesh,
        in_specs=(spec,) * 5,
        out_specs=(spec,) * 3,
        check_vma=False,
    )
```

time: 289 us -> 39.4 us (0.14)
  the two profiles are of different devices: /device:TPU:121 before, /device:TPU:79 now
where the time goes in v4:
time: 39.4 us; the launch traced here: 39.1 us
  Pallas kernels  38.5 us (98%)
  between operations  0.64 us (2%)
    pallas_call x1, Pallas kernels, body(): pl.pallas_call(functools.partial(kernel, slabs, bands, heads), out_shape=...  37.5 us
    pallas_call x1, Pallas kernels, body(): pl.pallas_call(store, out_shape=(out, out, out), in_specs=[vmem] * 3, out...  1.03 us

profile of v4, /device:TPU:79, one launch (start us, length us, event | category | flops | bytes accessed | tf_op | source)
XLA Modules:
  0.0 39.1 jit_solution(11844744433605518641)
XLA Ops:
  0.6 37.5 %shard_map.76 = (bf16[1,1,128,1536]{3,2,1,0:T(8,128)(2,1)S(1)}, bf16[1,1,128,1536]{3,2,1,0:T(8,128)(2,1)S(1)}, bf16[1,1,128,1536]{3,2,1,0:T(8,128)(2,1)S(1)}) custom-call(bf16[1,1,128,1536]{3,2,1,0:T(8,128)(2,1)} %q_hbm.1, bf16[1,1,128,1536]{3,2,1,0:T(8,128)(2,1)} %k_hbm.1, bf16[1,1,128,1536]{3,2,1,0:T(8,128)(2,1)} %v_hbm.1, ...), custom_call_target="tpu_custom_call" | custom-call | flops 1258291200 | bytes 2752512 | tf_op jit(solution)/shard_map/pallas_call | solution.py:512
  38.1 1.0 %shard_map.77 = (bf16[1,1,128,1536]{3,2,1,0:T(8,128)(2,1)}, bf16[1,1,128,1536]{3,2,1,0:T(8,128)(2,1)}, bf16[1,1,128,1536]{3,2,1,0:T(8,128)(2,1)}) custom-call(bf16[1,1,128,1536]{3,2,1,0:T(8,128)(2,1)S(1)} %get-tuple-element.6.a, bf16[1,1,128,1536]{3,2,1,0:T(8,128)(2,1)S(1)} %get-tuple-element.7.b, bf16[1,1,128,1536]{3,2,1,0:T(8,128)(2,1)S(1)} %get-tuple-element.8.c), custom_call_target="tpu_custom_call" | custom-call | tf_op jit(solution)/shard_map/pallas_call | solution.py:563

commit v5 on v4

--- a/solution.py
+++ b/solution.py
@@ -1,4 +1,5 @@
 import functools
+import itertools
 import math
 
 import jax
@@ -20,7 +21,7 @@
 G, H = 1, 2
 PAIRS = (OWN, C, X, Y, F)
 AHEAD = 3
-LAG_SCORES, LAG_COMBINE, LAG_GRADS, LAG_RETURN, LAG_FINAL = 1, 3, 5, 8, 12
+LAG_SCORES, LAG_GRADS, LAG_RETURN, LAG_FINAL = 1, 4, 8, 12
 
 
 def kernel(
@@ -44,11 +45,8 @@
     bias_out,
     bias_in,
     bias_x,
-    st_own,
     st_out,
     st_in,
-    fin_own,
-    fin_in,
     dq_own,
     dq_send,
     dq_in,
@@ -63,8 +61,6 @@
     arr_rsem,
     st_ssem,
     st_rsem,
-    fin_ssem,
-    fin_rsem,
     dq_ssem,
     dq_rsem,
     dkv_ssem,
@@ -82,10 +78,14 @@
     has_zout = (b_zout >= 0) & (b_zout < bands)
     bent = (t == slabs // 2 - 1) | (t == slabs // 2)
     straight = has_y & jnp.logical_not(bent)
+    t_cy, t_yc = t - 2 * tstep, t + 2 * tstep
+    c_bent = (t_c == slabs // 2 - 1) | (t_c == slabs // 2)
+    c_straight = (t_cy >= 0) & (t_cy < slabs) & jnp.logical_not(c_bent)
 
     partner = {C: (t_c, b), Y: (t_y, b), X: (t, b_x)}
     reached = {C: None, Y: straight, X: None}
     across, zout, zin = (t_y, b_x), (t, b_zout), (t, b_zin)
+    beside, c_y, y_c = (t_c, b_x), (t_cy, b), (t_yc, b)
 
     def guarded(condition, action):
         if condition is None:
@@ -122,7 +122,10 @@
         (partner[X], None),
         (partner[C], None),
         (partner[Y], straight),
-        (across, bent),
+        (across, has_y),
+        (beside, None),
+        (c_y, c_straight),
+        (y_c, straight),
         (zout, has_zout),
         (zin, has_f),
     ):
@@ -133,7 +136,8 @@
         start_load(h)
 
     window_load.start()
-    count = 2 + has_y.astype(jnp.int32) + has_f.astype(jnp.int32) + has_zout.astype(jnp.int32)
+    count = 3 + has_y.astype(jnp.int32) + has_f.astype(jnp.int32) + has_zout.astype(jnp.int32)
+    count = count + 2 * straight.astype(jnp.int32) + c_straight.astype(jnp.int32)
     pl.semaphore_wait(barrier, count)
 
     def remote(src, dst, send, recv, device):
@@ -162,6 +166,9 @@
 
     def send_own(h):
         send_x(h, 0)
+        send_rest(h)
+
+    def send_rest(h):
         recv = arr_rsem.at[h]
 
         @pl.when(has_f)
@@ -178,13 +185,28 @@
 
         remote(fw.at[OWN, h], fw.at[C, h], fwd_ssem.at[C], recv, partner[C]).start()
 
-    def send_st(n, h):
-        remote(
-            st_out.at[n, h], st_in.at[n, h], st_ssem.at[n], st_rsem.at[h], partner[n]
-        ).start()
-
-    def send_fin(n, h):
-        remote(fin_own.at[h], fin_in.at[n, h], fin_ssem.at[n], fin_rsem.at[h], partner[n]).start()
+    def send_st(n, at, device, group, h):
+        remote(st_out.at[n, h], st_in.at[at, h], st_ssem.at[group], st_rsem.at[h], device).start()
+
+    def send_parts(h):
+        send_st(2, 1, partner[X], 0, h)
+        send_st(0, 6, partner[X], 0, h)
+        send_st(2, 4, beside, 0, h)
+        send_st(1, 7, beside, 0, h)
+        send_st(1, 0, partner[C], 0, h)
+        send_st(0, 3, partner[C], 0, h)
+
+        @pl.when(straight)
+        def _():
+            send_st(2, 11, across, 1, h)
+            send_st(3, 8, across, 1, h)
+            send_st(3, 2, partner[Y], 1, h)
+            send_st(0, 9, partner[Y], 1, h)
+            send_st(3, 5, y_c, 1, h)
+
+        @pl.when(c_straight)
+        def _():
+            send_st(1, 10, c_y, 2, h)
 
     def send_dq(n, h):
         remote(
@@ -220,16 +242,13 @@
         def _():
             landed(buffer.at[pl.ds(1, 2), h], sem.at[h])
 
-    def to_reached(send, h):
-        for n in (X, Y, C):
-            guarded(reached[n], functools.partial(send, n, h))
-
     wait_load(0, AHEAD, 0)
 
     @pl.loop(0, AHEAD)
     def _(h):
-        send_own(h)
+        send_x(h, 0)
         send_x(h, 1)
+        send_rest(h)
 
     @pl.loop(AHEAD, heads)
     def _(h):
@@ -268,7 +287,16 @@
     for n in (X, C, Y):
         guarded(reached[n], lambda n=n: bias_copy(n).start())
 
-    zero_row = jnp.zeros((1, BLOCK), jnp.float32)
+    def blank_part(at, h):
+        st_in[at, h, 0] = jnp.full((1, BLOCK), MASKED, jnp.float32)
+        for row in (1, 2):
+            st_in[at, h, row] = jnp.zeros((1, BLOCK), jnp.float32)
+
+    @pl.when(jnp.logical_not(c_straight))
+    def _():
+        @pl.loop(0, heads)
+        def _(h):
+            blank_part(5, h)
 
     @pl.when(jnp.logical_not(straight))
     def _():
@@ -277,11 +305,8 @@
         @pl.loop(0, heads)
         def _(h):
             fw[Y, h] = jnp.zeros(fw.shape[2:], fw.dtype)
-            st_in[Y, h, 0] = jnp.full((1, BLOCK), MASKED, jnp.float32)
-            for at in (1, 2):
-                st_in[Y, h, at] = zero_row
-            for at in range(3):
-                fin_in[Y, h, at] = zero_row
+            for at in (2, 8, 9, 10, 11):
+                blank_part(at, h)
             dq_in[Y, h] = jnp.zeros(dq_in.shape[2:], dq_in.dtype)
 
     @pl.when(jnp.logical_not(has_zout))
@@ -356,50 +381,53 @@
             jnp.where(bent, row[Y], 0.0) for row in (total, mixed)
         )
         x_part = merged([part[X], part[F], y_part])
-        for at in range(3):
-            st_own[h, at] = part[OWN][at]
-            st_out[C, h, at] = part[C][at]
-            st_out[Y, h, at] = part[Y][at]
-            st_out[X, h, at] = x_part[at]
-        to_reached(send_st, h)
-
-    def stage_combine(h):
-        from_reached(st_in, h, st_rsem)
-        parts = [tuple(st_own[h, at] for at in range(3))]
-        parts += [tuple(st_in[n, h, at] for at in range(3)) for n in (C, Y, X)]
+        for slot, rows in enumerate((part[OWN], part[C], x_part, part[Y])):
+            for at in range(3):
+                st_out[slot, h, at] = rows[at]
+        send_parts(h)
+
+    def stage_grads(h):
+        for its, own in itertools.product((False, True), repeat=2):
+
+            @pl.when((c_straight == its) & (straight == own))
+            def _(its=its, own=own):
+                landed(st_in.at[pl.ds(0, 6 + 5 * own + its), h], st_rsem.at[h])
+
+        def side_by_side(ref, places, at):
+            return jnp.concatenate([ref[place, h, at] for place in places], axis=1)
+
+        parts = [tuple(side_by_side(st_out, range(4), at) for at in range(3))]
+        for sender in range(3):
+            places = range(sender, 12, 3)
+            parts.append(tuple(side_by_side(st_in, places, at) for at in range(3)))
         top, total, mixed = merged(parts)
         inverse = 1.0 / total
-        for at, row in enumerate((top, inverse, mixed * inverse)):
-            fin_own[h, at] = row
-        to_reached(send_fin, h)
-
-    def stage_grads(h):
-        from_reached(fin_in, h, fin_rsem)
-        top, inverse, delta = (
-            jnp.concatenate(
-                [
-                    fin_own[h, at],
-                    fin_in[C, h, at],
-                    fin_in[X, h, at],
-                    jnp.where(bent, fin_in[X, h, at], fin_in[Y, h, at]),
-                    fin_in[X, h, at],
-                ],
-                axis=1,
-            )
-            for at in range(3)
-        )
+
+        def for_pairs(row):
+            x_row, y_row = row[:, 2 * BLOCK : 3 * BLOCK], row[:, 3 * BLOCK :]
+            y_row = jnp.where(bent, x_row, y_row)
+            return jnp.concatenate([row[:, : 3 * BLOCK], y_row, x_row], axis=1)
+
+        top, inverse, delta = for_pairs(top), for_pairs(inverse), for_pairs(mixed * inverse)
         own_top = jnp.concatenate([tops[h, i] for i in range(5)], axis=1)
         factor = jnp.exp2((own_top - top) * SCALE_LOG2E) * inverse
         probs = weight[h] * factor
         grad_scores = (probs * ((gprob[h] - delta) * SCALE)).astype(jnp.bfloat16)
         probs = probs.astype(jnp.bfloat16)
         third, fourth = 3 * BLOCK, 4 * BLOCK
-        own_scores = grad_scores[:, :third]
-        y_scores = grad_scores[:, third:fourth]
-        g_scores = grad_scores[:, fourth:]
-        turned = dot(kv[OWN, h, 0], own_scores, 0, 0)
-        y_turned = dot(kv[y_keys, h, 0], y_scores, 0, 0)
-        g_turned = dot(kv[G, h, 0], g_scores, 0, 0)
+        lefts = (grad_scores, probs)
+        for piece, left in enumerate(lefts):
+            from_g = dot(left[:, fourth:], fw[X, h, piece], 1, 0)
+            dkv_send[0, h, piece] = from_g.astype(jnp.bfloat16)
+        guarded(has_zout, lambda: send_dkv(0, h, zout))
+        for piece, left in enumerate(lefts):
+            from_y = dot(left[:, third:fourth], fw[y_queries, h, piece], 1, 0)
+            dkv_send[1, h, piece] = from_y.astype(jnp.bfloat16)
+            dkv_own[h, piece] = jnp.where(bent, 0.0, from_y)
+        guarded(bent, lambda: send_dkv(1, h, across))
+        turned = dot(kv[OWN, h, 0], grad_scores[:, :third], 0, 0)
+        y_turned = dot(kv[y_keys, h, 0], grad_scores[:, third:fourth], 0, 0)
+        g_turned = dot(kv[G, h, 0], grad_scores[:, fourth:], 0, 0)
         dq_own[h] = turned[:, :BLOCK]
         dq_send[C, h] = turned[:, BLOCK : 2 * BLOCK].astype(jnp.bfloat16)
         dq_send[Y, h] = y_turned.astype(jnp.bfloat16)
@@ -407,15 +435,9 @@
         dq_send[X, h] = x_turned.astype(jnp.bfloat16)
         guarded(straight, lambda: send_dq(Y, h))
         send_dq(C, h)
-        for piece, left in enumerate((grad_scores, probs)):
+        for piece, left in enumerate(lefts):
             own = dot(left[:, :third], thrice(h, piece), 1, 0)
-            from_y = dot(left[:, third:fourth], fw[y_queries, h, piece], 1, 0)
-            from_g = dot(left[:, fourth:], fw[X, h, piece], 1, 0)
-            dkv_own[h, piece] = own + jnp.where(bent, 0.0, from_y)
-            dkv_send[0, h, piece] = from_g.astype(jnp.bfloat16)
-            dkv_send[1, h, piece] = from_y.astype(jnp.bfloat16)
-        guarded(has_zout, lambda: send_dkv(0, h, zout))
-        guarded(bent, lambda: send_dkv(1, h, across))
+            dkv_own[h, piece] = dkv_own[h, piece] + own
 
     def stage_return(h):
         send_dq(X, h)
@@ -449,7 +471,6 @@
     stages = (
         (0, stage_arrival),
         (LAG_SCORES, stage_scores),
-        (LAG_COMBINE, stage_combine),
         (0, stage_second_piece),
         (LAG_FINAL, stage_final),
         (LAG_RETURN, stage_return),
@@ -481,12 +502,15 @@
 
     def wait_sends(n):
         sent(bias_out if n == X else bias_out.at[n], bias_ssem.at[n])
-        sent(st_out.at[n], st_ssem.at[n])
-        sent(fin_own, fin_ssem.at[n])
         sent(dq_send.at[n], dq_ssem.at[n])
 
     for n in (C, Y, X):
         guarded(reached[n], functools.partial(wait_sends, n))
+    for group, (parts, condition) in enumerate(((6, None), (5, straight), (1, c_straight))):
+        guarded(
+            condition,
+            lambda group=group, parts=parts: sent(st_in.at[pl.ds(0, parts)], st_ssem.at[group]),
+        )
     guarded(has_zout, lambda: sent(dkv_send.at[0], dkv_ssem.at[0]))
     guarded(bent, lambda: sent(dkv_send.at[1], dkv_ssem.at[1]))
 
@@ -524,11 +548,8 @@
             pltpu.VMEM((5, 2, 1, BLOCK), f32),
             pltpu.VMEM((3, 2, 1, BLOCK), f32),
             pltpu.VMEM((5, 2, 1, BLOCK), f32),
-            pltpu.VMEM((heads, 3, 1, BLOCK), f32),
             pltpu.VMEM((4, heads, 3, 1, BLOCK), f32),
-            pltpu.VMEM((4, heads, 3, 1, BLOCK), f32),
-            pltpu.VMEM((heads, 3, 1, BLOCK), f32),
-            pltpu.VMEM((4, heads, 3, 1, BLOCK), f32),
+            pltpu.VMEM((12, heads, 3, 1, BLOCK), f32),
             pltpu.VMEM((heads, HEAD_DIM, BLOCK), f32),
             pltpu.VMEM((4, heads, HEAD_DIM, BLOCK), bf16),
             pltpu.VMEM((4, heads, HEAD_DIM, BLOCK), bf16),
@@ -541,9 +562,7 @@
             dma((5,)),
             dma((heads,)),
             dma((heads,)),
-            dma((4,)),
-            dma((heads,)),
-            dma((4,)),
+            dma((3,)),
             dma((heads,)),
             dma((4,)),
             dma((heads,)),

time: 39.4 us -> 38.6 us (0.980)
  the two profiles are of different devices: /device:TPU:79 before, /device:TPU:1 now
where the time goes in v5:
time: 38.6 us; the launch traced here: 38.4 us
  Pallas kernels  37.7 us (98%)
  between operations  0.64 us (2%)
    pallas_call x1, Pallas kernels, body(): pl.pallas_call(functools.partial(kernel, slabs, bands, heads), out_shape=...  36.7 us
    pallas_call x1, Pallas kernels, body(): pl.pallas_call(store, out_shape=(out, out, out), in_specs=[vmem] * 3, out...  1.03 us

profile of v5, /device:TPU:1, one launch (start us, length us, event | category | flops | bytes accessed | tf_op | source)
XLA Modules:
  0.0 38.4 jit_solution(898686794964633526)
XLA Ops:
  0.6 36.7 %shard_map.76 = (bf16[1,1,128,1536]{3,2,1,0:T(8,128)(2,1)S(1)}, bf16[1,1,128,1536]{3,2,1,0:T(8,128)(2,1)S(1)}, bf16[1,1,128,1536]{3,2,1,0:T(8,128)(2,1)S(1)}) custom-call(bf16[1,1,128,1536]{3,2,1,0:T(8,128)(2,1)} %q_hbm.1, bf16[1,1,128,1536]{3,2,1,0:T(8,128)(2,1)} %k_hbm.1, bf16[1,1,128,1536]{3,2,1,0:T(8,128)(2,1)} %v_hbm.1, ...), custom_call_target="tpu_custom_call" | custom-call | flops 1258291200 | bytes 2752512 | tf_op jit(solution)/shard_map/pallas_call | solution.py:536
  37.3 1.0 %shard_map.77 = (bf16[1,1,128,1536]{3,2,1,0:T(8,128)(2,1)}, bf16[1,1,128,1536]{3,2,1,0:T(8,128)(2,1)}, bf16[1,1,128,1536]{3,2,1,0:T(8,128)(2,1)}) custom-call(bf16[1,1,128,1536]{3,2,1,0:T(8,128)(2,1)S(1)} %get-tuple-element.6.a, bf16[1,1,128,1536]{3,2,1,0:T(8,128)(2,1)S(1)} %get-tuple-element.7.b, bf16[1,1,128,1536]{3,2,1,0:T(8,128)(2,1)S(1)} %get-tuple-element.8.c), custom_call_target="tpu_custom_call" | custom-call | tf_op jit(solution)/shard_map/pallas_call | solution.py:582

commit v6 on v5

--- a/solution.py
+++ b/solution.py
@@ -64,7 +64,6 @@
     dq_ssem,
     dq_rsem,
     dkv_ssem,
-    dkv_rsem,
 ):
     t = lax.axis_index("tm")
     b = lax.axis_index("space")
@@ -215,7 +214,7 @@
 
     def send_dkv(at, h, device):
         remote(
-            dkv_send.at[at, h], dkv_in.at[at, h], dkv_ssem.at[at], dkv_rsem.at[h], device
+            dkv_send.at[at, h], dkv_in.at[at, h], dkv_ssem.at[at], dq_rsem.at[h], device
         ).start()
 
     def landed(span, sem):
@@ -443,12 +442,18 @@
         send_dq(X, h)
 
     def stage_final(h):
-        from_reached(dq_in, h, dq_rsem)
+        for more, terms in itertools.product((2, 3), range(3)):
+            one, two = has_f != bent, has_f & bent
+            pairs = (jnp.logical_not(has_f | bent), one, two)[terms]
+
+            @pl.when(pairs & (straight == (more == 3)))
+            def _(count=more + 2 * terms):
+                landed(fw.at[0, pl.ds(0, count), 0], dq_rsem.at[h])
+
         total = dq_own[h]
         for n in (C, Y, X):
             total = total + dq_in[n, h].astype(jnp.float32)
         dq_out[0, 0, :, cols(h)] = total.T.astype(jnp.bfloat16)
-        by_count(0, has_f, bent, lambda count: landed(dkv_in.at[pl.ds(0, count), h], dkv_rsem.at[h]))
         for piece, out in enumerate((dk_out, dv_out)):
             total = dkv_own[h, piece]
             for at in range(2):
@@ -470,8 +475,8 @@
     wait_load(AHEAD, heads, 1)
     stages = (
         (0, stage_arrival),
+        (0, stage_second_piece),
         (LAG_SCORES, stage_scores),
-        (0, stage_second_piece),
         (LAG_FINAL, stage_final),
         (LAG_RETURN, stage_return),
         (LAG_GRADS, stage_grads),
@@ -567,7 +572,6 @@
             dma((4,)),
             dma((heads,)),
             dma((2,)),
-            dma((heads,)),
         ],
         compiler_params=pltpu.CompilerParams(
             collective_id=0, has_side_effects=True, vmem_limit_bytes=58 << 20

time: 38.6 us -> 38.1 us (0.987)
  the two profiles are of different devices: /device:TPU:1 before, /device:TPU:120 now
where the time goes in v6:
time: 38.1 us; the launch traced here: 37.9 us
  Pallas kernels  37.2 us (98%)
  between operations  0.64 us (2%)
    pallas_call x1, Pallas kernels, body(): pl.pallas_call(functools.partial(kernel, slabs, bands, heads), out_shape=...  36.2 us
    pallas_call x1, Pallas kernels, body(): pl.pallas_call(store, out_shape=(out, out, out), in_specs=[vmem] * 3, out...  1.03 us

profile of v6, /device:TPU:120, one launch (start us, length us, event | category | flops | bytes accessed | tf_op | source)
XLA Modules:
  0.0 37.9 jit_solution(14705288868839179769)
XLA Ops:
  0.6 36.2 %shard_map.76 = (bf16[1,1,128,1536]{3,2,1,0:T(8,128)(2,1)S(1)}, bf16[1,1,128,1536]{3,2,1,0:T(8,128)(2,1)S(1)}, bf16[1,1,128,1536]{3,2,1,0:T(8,128)(2,1)S(1)}) custom-call(bf16[1,1,128,1536]{3,2,1,0:T(8,128)(2,1)} %q_hbm.1, bf16[1,1,128,1536]{3,2,1,0:T(8,128)(2,1)} %k_hbm.1, bf16[1,1,128,1536]{3,2,1,0:T(8,128)(2,1)} %v_hbm.1, ...), custom_call_target="tpu_custom_call" | custom-call | flops 1258291200 | bytes 2752512 | tf_op jit(solution)/shard_map/pallas_call | solution.py:541
  36.8 1.0 %shard_map.77 = (bf16[1,1,128,1536]{3,2,1,0:T(8,128)(2,1)}, bf16[1,1,128,1536]{3,2,1,0:T(8,128)(2,1)}, bf16[1,1,128,1536]{3,2,1,0:T(8,128)(2,1)}) custom-call(bf16[1,1,128,1536]{3,2,1,0:T(8,128)(2,1)S(1)} %get-tuple-element.6.a, bf16[1,1,128,1536]{3,2,1,0:T(8,128)(2,1)S(1)} %get-tuple-element.7.b, bf16[1,1,128,1536]{3,2,1,0:T(8,128)(2,1)S(1)} %get-tuple-element.8.c), custom_call_target="tpu_custom_call" | custom-call | tf_op jit(solution)/shard_map/pallas_call | solution.py:586
